TPU v7x, 32 devices: a whole 2x2x4 slice. The times are simulated.
32 devices in a mesh: gx: 4 (over y, core), gy: 8 (over z, x).
Axes of the slice: x: 2, y: 2, z: 4, core: 2. Of those that a mesh axis runs over, the one named last changes fastest.
Arguments:
- velocity: float32 [3, 32, 64, 512], P(None, 'gx', 'gy'), may hold values from -6 to 6
- stress: float32 [6, 32, 64, 512], P(None, 'gx', 'gy'), may hold values from -6 to 6
- lame_lambda: float32 [32, 64, 512], P('gx', 'gy'), may hold values from 0.5 to 5
- lame_mu: float32 [32, 64, 512], P('gx', 'gy'), may hold values from 0.5 to 5
- node_mass: float32 [32, 64, 512], P('gx', 'gy'), may hold values from 0.5 to 2
- displacement: float32 [3, 32, 64, 512], P(None, 'gx', 'gy'), may hold values from -0.75 to 0.75
- seg_elem: int32 [65536], P(('gx', 'gy')), may hold values from 0 to 32767
- seg_bucket: int32 [65536, 1], P(('gx', 'gy')), may hold values from 0 to 31; in each aligned block of 2048 rows (0 to 2047, 2048 to 4095, ...) at most 128 rows name the same one
- slave_points: float32 [3, 16384], P(None, ('gx', 'gy')), may hold values from 0.8 to 1.2
- candidates: int32 [4, 16384], P(None, ('gx', 'gy')), may hold values from 0 to 4095
Outputs:
- new_stress: float32 [6, 32, 64, 512], P(None, 'gx', 'gy')
- acceleration: float32 [3, 32, 64, 512], P(None, 'gx', 'gy')
- slave_force: float32 [3, 16384], P(None, ('gx', 'gy'))
Inputs may be any that keep to these rules, and one draw needn't show every extreme that they name: `seg_bucket`: in the rows of one device no bucket is named more than 128 times. `candidates`: A slot index into the 32 x 128 segment slots of the slave's own bucket, source device major; a slot holding no segment contributes nothing.
All inputs are finite; a program needn't handle non-finite values.
Results may differ from a plain program's by a relative error of at most 0.0003.
Values sent between devices are 32-bit elements; how exact they have to be, the bound alone decides.
A program may use at most 128 MiB of HBM per device.

v0:
```python
import jax
import jax.numpy as jnp
from jax import lax
from jax.sharding import PartitionSpec as P

time_step = 0.1
penalty = 10.0


def shifted(array, axis, by):
    size = lax.axis_size(axis)
    pairs = [(i, i + by) for i in range(size) if 0 <= i + by < size]
    return lax.ppermute(array, axis, pairs)


def element_pass(extended, stress, lame_lambda, lame_mu):
    size_x = extended.shape[1] - 1
    size_y = extended.shape[2] - 1
    size_z = extended.shape[3] - 1
    nodal = extended[0:3]

    def corner_vel(side_x, side_y, side_z):
        return nodal[
            :, side_x : side_x + size_x, side_y : side_y + size_y, side_z : side_z + size_z
        ]

    grad_x = 0.25 * sum((corner_vel(1, p, q) - corner_vel(0, p, q) for p in (0, 1) for q in (0, 1)))
    grad_y = 0.25 * sum((corner_vel(p, 1, q) - corner_vel(p, 0, q) for p in (0, 1) for q in (0, 1)))
    grad_z = 0.25 * sum((corner_vel(p, q, 1) - corner_vel(p, q, 0) for p in (0, 1) for q in (0, 1)))
    rate_xx = grad_x[0]
    rate_yy = grad_y[1]
    rate_zz = grad_z[2]
    rate_yz = 0.5 * (grad_z[1] + grad_y[2])
    rate_xz = 0.5 * (grad_z[0] + grad_x[2])
    rate_xy = 0.5 * (grad_y[0] + grad_x[1])
    volume_rate = rate_xx + rate_yy + rate_zz
    stress_xx = stress[0] + time_step * (lame_lambda * volume_rate + 2.0 * lame_mu * rate_xx)
    stress_yy = stress[1] + time_step * (lame_lambda * volume_rate + 2.0 * lame_mu * rate_yy)
    stress_zz = stress[2] + time_step * (lame_lambda * volume_rate + 2.0 * lame_mu * rate_zz)
    stress_yz = stress[3] + time_step * 2.0 * lame_mu * rate_yz
    stress_xz = stress[4] + time_step * 2.0 * lame_mu * rate_xz
    stress_xy = stress[5] + time_step * 2.0 * lame_mu * rate_xy
    new_stress = jnp.stack([stress_xx, stress_yy, stress_zz, stress_yz, stress_xz, stress_xy])
    tensor = (
        (stress_xx, stress_xy, stress_xz),
        (stress_xy, stress_yy, stress_yz),
        (stress_xz, stress_yz, stress_zz),
    )
    forces = jnp.zeros((3, size_x + 1, size_y + 1, size_z + 1), extended.dtype)
    for side_x in (0, 1):
        for side_y in (0, 1):
            for side_z in (0, 1):
                sign_x = 2.0 * side_x - 1.0
                sign_y = 2.0 * side_y - 1.0
                sign_z = 2.0 * side_z - 1.0
                part = jnp.stack(
                    [
                        -0.25
                        * (
                            sign_x * tensor[row][0]
                            + sign_y * tensor[row][1]
                            + sign_z * tensor[row][2]
                        )
                        for row in range(3)
                    ]
                )
                forces = forces + jnp.pad(
                    part, ((0, 0), (side_x, 1 - side_x), (side_y, 1 - side_y), (side_z, 1 - side_z))
                )
    return (new_stress, forces)


def seg_geometry(corners):
    low_low = corners[0:3]
    high_low = corners[3:6]
    high_high = corners[6:9]
    low_high = corners[9:12]
    centre = 0.25 * (low_low + high_low + high_high + low_high)
    first = high_high - low_low
    second = low_high - high_low
    area = 0.5 * jnp.stack(
        [
            first[1] * second[2] - first[2] * second[1],
            first[2] * second[0] - first[0] * second[2],
            first[0] * second[1] - first[1] * second[0],
        ]
    )
    return (centre, area)


def slot_rank(bucket, devices):
    onehot = (bucket[:, None] == jnp.arange(devices, dtype=jnp.int32)[None, :]).astype(jnp.int32)
    running = jnp.cumsum(onehot, axis=0)
    return jnp.sum(running * onehot, axis=1) - 1


def per_device(
    velocity,
    stress,
    lame_lambda,
    lame_mu,
    node_mass,
    displacement,
    seg_elem,
    seg_bucket,
    slave_points,
    candidates,
):
    count_x = lax.axis_size("gx")
    count_y = lax.axis_size("gy")
    devices = count_x * count_y
    size_x = velocity.shape[1]
    size_y = velocity.shape[2]
    size_z = velocity.shape[3]
    seg_count = seg_elem.shape[0]
    capacity = 2 * seg_count // devices
    slots = devices * capacity
    own = jnp.concatenate([velocity, displacement], 0)
    ghost_x = shifted(own[:, :1], "gx", -1)
    extended = jnp.concatenate([own, ghost_x], 1)
    ghost_y = shifted(extended[:, :, :1], "gy", -1)
    extended = jnp.concatenate([extended, ghost_y], 2)
    extended = jnp.pad(extended, ((0, 0), (0, 0), (0, 0), (0, 1)))
    new_stress, forces = element_pass(extended, stress, lame_lambda, lame_mu)
    bucket = seg_bucket[:, 0]
    ranks = slot_rank(bucket, devices)
    target = bucket * capacity + ranks
    cell_i = seg_elem // (size_y * size_z)
    cell_j = seg_elem // size_z % size_y
    cell_k = seg_elem % size_z
    flat_disp = extended[3:6].reshape(3, -1)
    offsets = ((0, 0), (1, 0), (1, 1), (0, 1))
    indices = []
    pieces = []
    for off_a, off_b in offsets:
        index = ((cell_i + off_a) * (size_y + 1) + cell_j + off_b) * (size_z + 1) + cell_k + 1
        indices.append(index)
        shift_vec = jnp.array([off_a, off_b, 1.0], jnp.float32)[:, None]
        pieces.append(flat_disp[:, index] + shift_vec)
    corners = jnp.concatenate(pieces, 0)
    centre_own, area_own = seg_geometry(corners)
    payload = jnp.concatenate([centre_own, area_own], 0)
    width = payload.shape[0]
    outgoing = jnp.zeros((width, slots), jnp.float32).at[:, target].set(payload)
    arrived = lax.all_to_all(
        outgoing.reshape(width, devices, capacity),
        ("gx", "gy"),
        split_axis=1,
        concat_axis=1,
        tiled=True,
    )
    arrived = arrived.reshape(width, slots)
    centre = arrived[0:3]
    area = arrived[3:6]
    flat_candidates = candidates.reshape(-1)
    table = jnp.concatenate([centre, area], 0)
    near = table[:, flat_candidates].reshape(6, candidates.shape[0], candidates.shape[1])
    near_centre = near[0:3]
    near_area = near[3:6]
    gap = jnp.sum(near_area * (slave_points[:, None, :] - near_centre), axis=0)
    push = penalty * jnp.maximum(-gap, 0.0)[None] * near_area
    slave_force = jnp.sum(push, axis=1)
    reaction = jnp.zeros((3, slots), jnp.float32).at[:, flat_candidates].add(-push.reshape(3, -1))
    returned = lax.all_to_all(
        reaction.reshape(3, devices, capacity),
        ("gx", "gy"),
        split_axis=1,
        concat_axis=1,
        tiled=True,
    )
    returned = returned.reshape(3, slots)
    quarter = 0.25 * returned[:, target]
    flat_forces = forces.reshape(3, -1)
    for index in indices:
        flat_forces = flat_forces.at[:, index].add(quarter)
    forces = flat_forces.reshape(forces.shape)[:, :, :, :size_z]
    upper_y = shifted(forces[:, :, size_y : size_y + 1], "gy", 1)
    forces = forces[:, :, :size_y] + jnp.pad(upper_y, ((0, 0), (0, 0), (0, size_y - 1), (0, 0)))
    upper_x = shifted(forces[:, size_x : size_x + 1], "gx", 1)
    forces = forces[:, :size_x] + jnp.pad(upper_x, ((0, 0), (0, size_x - 1), (0, 0), (0, 0)))
    acceleration = forces / node_mass[None]
    return (new_stress, acceleration, slave_force)


def solution(mesh):
    return jax.shard_map(
        per_device,
        mesh=mesh,
        in_specs=(
            P(None, "gx", "gy", None),
            P(None, "gx", "gy", None),
            P("gx", "gy", None),
            P("gx", "gy", None),
            P("gx", "gy", None),
            P(None, "gx", "gy", None),
            P(("gx", "gy")),
            P(("gx", "gy"), None),
            P(None, ("gx", "gy")),
            P(None, ("gx", "gy")),
        ),
        out_specs=(P(None, "gx", "gy", None), P(None, "gx", "gy", None), P(None, ("gx", "gy"))),
        check_vma=False,
    )
```

profile of v0, /device:TPU:9, one launch (start us, length us, event | category | flops | bytes accessed | tf_op | source)
XLA Modules:
  0.0 285.8 jit_solution(2993142969272704066)
XLA Ops:
  0.7 1.0 constant_dynamic-update-slice_fusion.1
  1.7 1.0 constant_dynamic-update-slice_fusion
  2.7 2.6 collective-permute-start
  5.4 9.1 %reduce-window.6 = s32[32,16,128]{2,1,0:T(8,128)S(1)} reduce-window(s32[32,16,128]{2,1,0:T(8,128)S(1)} %fusion.32, s32[]{:T(128)} %constant.89.clone.1), window={size=1x1x128 pad=0_0x0_0x127_0}, to_apply=%region_0.1 | reduce-window | flops 8323072 | bytes 524292 | tf_op jit(solution)/shard_map/reduce-window
  15.4 0.6 broadcast_clamp_fusion.4
  16.1 3.0 %collective-permute-start.1 = (f32[6,9,1,512]{3,2,1,0:T(1,128)S(1)}, f32[6,9,1,512]{3,2,1,0:T(1,128)S(1)}, u32[]{:S(2)}, u32[]{:S(2)}) collective-permute-start(f32[6,9,1,512]{3,2,1,0:T(1,128)S(1)} %pad_maximum_fusion.3), channel_id=1, source_target_pairs={{1,0},{2,1},{3,2},{4,3},{5,4},{6,5},{7,6},{9,8},{10,9},{11,10},{12... | collective-permute-start | bytes 331784 | tf_op jit(solution)/shard_map/ppermute | solution.py:13
  19.2 0.9 copy.67
  20.0 2.8 collective-permute-done.1
  23.1 0.9 copy-done.1
  24.5 0.9 add_multiply_fusion.1
  25.4 0.7 reshape.123
  26.4 1.9 multiply_bitcast_fusion.23
  28.4 1.1 multiply_bitcast_fusion.20
  29.5 1.1 multiply_bitcast_fusion.19
  30.6 1.0 multiply_bitcast_fusion.18
  31.6 10.6 %copy.56 = f32[3,41553]{0,1:T(8,128)} copy(f32[3,41553]{1,0:T(4,128)S(1)} %reshape.123) | data formatting | bytes 997272 | tf_op jit(solution)/shard_map/reshape | solution.py:131
  42.3 12.5 %gather_fusion.3 = f32[2048,3]{1,0:T(8,128)S(1)} fusion(f32[3,41553]{0,1:T(8,128)} %copy.56, s32[2048]{0:T(1024)S(1)} %get-tuple-element.69), kind=kCustom, calls=%fused_computation.3 | custom fusion | bytes 57344 | tf_op jit(solution)/shard_map/gather | solution.py:139
  55.1 12.5 %gather_fusion.2 = f32[2048,3]{1,0:T(8,128)S(1)} fusion(f32[3,41553]{0,1:T(8,128)} %copy.56, s32[2048]{0:T(1024)S(1)} %get-tuple-element.67), kind=kCustom, calls=%fused_computation.2 | custom fusion | bytes 57344 | tf_op jit(solution)/shard_map/gather | solution.py:139
  68.0 12.5 %gather_fusion.1 = f32[2048,3]{1,0:T(8,128)S(1)} fusion(f32[3,41553]{0,1:T(8,128)} %copy.56, s32[2048]{0:T(1024)S(1)} %get-tuple-element.9), kind=kCustom, calls=%fused_computation.1 | custom fusion | bytes 57344 | tf_op jit(solution)/shard_map/gather | solution.py:139
  80.6 12.5 %gather_fusion = f32[2048,3]{1,0:T(8,128)S(1)} fusion(f32[3,41553]{0,1:T(8,128)} %copy.56, s32[2048]{0:T(1024)S(1)} %get-tuple-element.71), kind=kCustom, calls=%fused_computation | custom fusion | bytes 57344 | tf_op jit(solution)/shard_map/gather | solution.py:139
  94.4 6.2 %scatter_custom_fusion = f32[6,4096]{0,1:T(8,128)S(1)} fusion(s32[2048]{0:T(1024)} %bitcast.195, f32[2048,6]{1,0:T(8,128)S(1)} %copy.64, f32[]{:T(128)} %constant.80.clone.1), kind=kCustom, calls=%fused_computation.63 | custom fusion | bytes 98816 | tf_op jit(solution)/shard_map/scatter | solution.py:144
  100.7 1.3 copy.65
  102.0 6.3 %all-to-all-start = ((f32[6,32,128]{2,0,1:T(8,128)}), f32[6,32,128]{2,0,1:T(8,128)S(1)}, u32[]{:S(2)}, u32[]{:S(2)}) async-start(f32[6,32,128]{2,0,1:T(8,128)} %copy.65), calls=%async_computation | async-start | bytes 262144 | tf_op jit(solution)/shard_map/all_to_all | solution.py:145
  108.3 5.1 %fusion = f32[3,9,9,513]{3,2,1,0:T(8,128)} fusion(f32[1,8,8,512]{3,2,1,0:T(8,128)} %get-tuple-element.50, f32[1,8,8,512]{3,2,1,0:T(8,128)} %get-tuple-element.44, f32[1,8,8,512]{3,2,1,0:T(8,128)S(1)} %copy-done.9, f32[1,8,8,512]{3,2,1,0:T(8,128)} %get-tuple-element.49, f32[1,8,8,512]{3,2,1,0:T(8,128)} %get-tuple-element.43, ...), kind=kLoop, calls=%fused_computation.19 | loop fusion | flops 14086467 | bytes 3644364 | tf_op jit(solution)/shard_map/add | solution.py:67
  113.5 0.7 bitcast_dynamic-update-slice_fusion.2
  114.1 0.6 all-to-all-done
  114.8 0.6 copy.66
  115.5 5.5 %gather_fusion.4 = f32[2048,6]{1,0:T(8,128)S(1)} fusion(f32[6,4096]{0,1:T(8,128)S(1)} %copy.66, s32[2048]{0:T(1024)S(1)} %get-tuple-element.73), kind=kCustom, calls=%fused_computation.4 | custom fusion | bytes 106496 | tf_op jit(solution)/shard_map/gather | solution.py:157
  120.9 2.3 fusion.54
  123.2 13.1 %scatter_custom_fusion.1 = f32[3,4096]{0,1:T(8,128)S(1)} fusion(s32[2048]{0:T(1024)} %bitcast.199, f32[]{:T(128)} %constant.80.clone.1, f32[2048]{0:T(1024)S(1)} %maximum_multiply_fusion.1, f32[6,2048]{0,1:T(8,128)S(1)} %bitcast.184), kind=kCustom, calls=%fused_computation.58 | custom fusion | flops 18432 | bytes 107008 | tf_op jit(solution)/shard_map/scatter-add | solution.py:163
  136.4 1.2 copy.68
  137.6 5.2 %all-to-all-start.1 = ((f32[3,32,128]{2,0,1:T(4,128)}), f32[3,32,128]{2,0,1:T(4,128)S(1)}, u32[]{:S(2)}, u32[]{:S(2)}) async-start(f32[3,32,128]{2,0,1:T(4,128)} %copy.68), calls=%async_computation.1 | async-start | bytes 131072 | tf_op jit(solution)/shard_map/all_to_all | solution.py:164
  142.8 0.7 bitcast_dynamic-update-slice_fusion.1
  143.5 1.9 reshape.120
  145.4 10.6 %copy.70 = f32[3,41553]{0,1:T(8,128)} copy(f32[3,41553]{1,0:T(4,128)S(1)} %reshape.120) | data formatting | bytes 997272 | tf_op jit(solution)/shard_map/reshape | solution.py:173
  156.0 0.6 copy.69
  156.7 5.5 %gather_fusion.5 = f32[2048,3]{1,0:T(8,128)S(1)} fusion(f32[3,4096]{0,1:T(8,128)S(1)} %bitcast.188, s32[2048]{0:T(1024)S(1)} %broadcast_clamp_fusion), kind=kCustom, calls=%fused_computation.5 | custom fusion | bytes 57344 | tf_op jit(solution)/shard_map/gather | solution.py:172
  162.2 24.6 %scatter_custom_fusion.2 = f32[3,41553]{0,1:T(8,128)} fusion(f32[3,41553]{0,1:T(8,128)} %copy.70, s32[2048]{0:T(1024)} %get-tuple-element.72, f32[2048,3]{1,0:T(8,128)S(1)} %gather_fusion.5, f32[]{:T(128)} %constant.81.clone.1), kind=kCustom, calls=%fused_computation.70 | custom fusion | flops 12288 | bytes 523724 | tf_op jit(solution)/shard_map/scatter-add | solution.py:175
  186.8 24.6 %scatter_custom_fusion.3 = f32[3,41553]{0,1:T(8,128)} fusion(f32[3,41553]{0,1:T(8,128)} %scatter_custom_fusion.2, s32[2048]{0:T(1024)} %get-tuple-element.10, f32[2048,3]{1,0:T(8,128)S(1)} %gather_fusion.5, f32[]{:T(128)} %constant.81.clone.1), kind=kCustom, calls=%fused_computation.68 | custom fusion | flops 12288 | bytes 523724 | tf_op jit(solution)/shard_map/scatter-add | solution.py:175
  211.4 24.6 %scatter_custom_fusion.4 = f32[3,41553]{0,1:T(8,128)} fusion(f32[3,41553]{0,1:T(8,128)} %scatter_custom_fusion.3, s32[2048]{0:T(1024)} %get-tuple-element.68, f32[2048,3]{1,0:T(8,128)S(1)} %gather_fusion.5, f32[]{:T(128)} %constant.81.clone.1), kind=kCustom, calls=%fused_computation.66 | custom fusion | flops 12288 | bytes 523724 | tf_op jit(solution)/shard_map/scatter-add | solution.py:175
  236.0 24.6 %scatter_custom_fusion.5 = f32[3,41553]{0,1:T(8,128)} fusion(f32[3,41553]{0,1:T(8,128)} %scatter_custom_fusion.4, s32[2048]{0:T(1024)} %get-tuple-element.70, f32[2048,3]{1,0:T(8,128)S(1)} %gather_fusion.5, f32[]{:T(128)} %constant.81.clone.1), kind=kCustom, calls=%fused_computation.72 | custom fusion | flops 12288 | bytes 523724 | tf_op jit(solution)/shard_map/scatter-add | solution.py:175
  260.7 12.0 %copy.71 = f32[3,41553]{1,0:T(4,128)S(1)} copy(f32[3,41553]{0,1:T(8,128)} %scatter_custom_fusion.5) | data formatting | bytes 997272 | tf_op jit(solution)/shard_map/scatter-add | solution.py:175
  273.3 3.2 %collective-permute-start.2 = (f32[3,9,1,512]{3,2,1,0:T(1,128)S(1)}, f32[3,9,1,512]{3,2,1,0:T(1,128)S(1)}, u32[]{:S(2)}, u32[]{:S(2)}) collective-permute-start(f32[3,9,1,512]{3,2,1,0:T(1,128)S(1)} %slice.256), channel_id=1, source_target_pairs={{0,1},{1,2},{2,3},{3,4},{4,5},{5,6},{6,7},{8,9},{9,10},{10,11},{11... | collective-permute-start | bytes 165896 | tf_op jit(solution)/shard_map/ppermute | solution.py:13
  276.5 0.7 bitcast_dynamic-update-slice_fusion
  277.2 2.0 collective-permute-done.2
  279.3 4.5 %collective-permute-start.3 = (f32[3,1,8,512]{3,2,1,0:T(8,128)S(1)}, f32[3,1,8,512]{3,2,1,0:T(8,128)S(1)}, u32[]{:S(2)}, u32[]{:S(2)}) collective-permute-start(f32[3,1,8,512]{3,2,1,0:T(8,128)S(1)} %slice.258), channel_id=1, source_target_pairs={{0,8},{8,16},{16,24},{1,9},{9,17},{17,25},{2,10},{10,18},{18,26},{... | collective-permute-start | bytes 147464 | tf_op jit(solution)/shard_map/ppermute | solution.py:13
  284.2 0.7 copy.72
  285.0 0.8 fusion.29
  (88 shorter events, 5.3 us)
Async XLA Ops:
  0.6 4.7 %copy-start.19 = (s32[4,512]{1,0:T(4,128)S(1)}, s32[4,512]{1,0:T(4,128)}, u32[]{:S(2)}) copy-start(s32[4,512]{1,0:T(4,128)} %param.23) | copy-start | bytes 24580
  0.6 4.7 %copy-start.14 = (s32[2048,1]{0,1:T(1,128)S(1)}, s32[2048,1]{0,1:T(1,128)}, u32[]{:S(2)}) copy-start(s32[2048,1]{0,1:T(1,128)} %param.21) | copy-start | bytes 24580
  2.7 13.3 %collective-permute-start = (f32[6,1,8,512]{3,2,1,0:T(8,128)S(1)}, f32[6,1,8,512]{3,2,1,0:T(8,128)S(1)}, u32[]{:S(2)}, u32[]{:S(2)}) collective-permute-start(f32[6,1,8,512]{3,2,1,0:T(8,128)S(1)} %slice.231), channel_id=1, source_target_pairs={{8,0},{16,8},{24,16},{9,1},{17,9},{25,17},{10,2},{18,10},{26,18},{... | collective-permute-start | bytes 294920 | tf_op jit(solution)/shard_map/ppermute | solution.py:13
  5.4 10.0 %copy-start.16 = (s32[2048,1]{0,1:T(1,128)}, s32[2048,1]{0,1:T(1,128)S(1)}, u32[]{:S(2)}) copy-start(s32[2048,1]{0,1:T(1,128)S(1)} %compare_select_fusion.1) | copy-start | bytes 24580
  5.4 10.0 %copy-start.20 = (s32[2048]{0:T(1024)S(1)}, s32[2048]{0:T(1024)}, u32[]{:S(2)}) copy-start(s32[2048]{0:T(1024)} %param.20) | copy-start | bytes 24580
  14.6 4.5 %copy-start.18 = (f32[3,512]{1,0:T(4,128)S(1)}, f32[3,512]{1,0:T(4,128)}, u32[]{:S(2)}) copy-start(f32[3,512]{1,0:T(4,128)} %param.22) | copy-start | bytes 18436
  15.4 7.6 %copy-start.15 = (s32[2048,1]{0,1:T(1,128)}, s32[2048,1]{0,1:T(1,128)S(1)}, u32[]{:S(2)}) copy-start(s32[2048,1]{0,1:T(1,128)S(1)} %compare_select_fusion) | copy-start | bytes 24580
  16.1 6.7 %collective-permute-start.1 = (f32[6,9,1,512]{3,2,1,0:T(1,128)S(1)}, f32[6,9,1,512]{3,2,1,0:T(1,128)S(1)}, u32[]{:S(2)}, u32[]{:S(2)}) collective-permute-start(f32[6,9,1,512]{3,2,1,0:T(1,128)S(1)} %pad_maximum_fusion.3), channel_id=1, source_target_pairs={{1,0},{2,1},{3,2},{4,3},{5,4},{6,5},{7,6},{9,8},{10,9},{11,10},{12... | collective-permute-start | bytes 331784 | tf_op jit(solution)/shard_map/ppermute | solution.py:13
  23.0 1.0 copy-start.1
  25.4 0.9 copy-start.2
  25.4 1.0 copy-start.12
  26.4 2.0 copy-start.3
  31.6 10.6 %copy-start.17 = (f32[6,8,8,512]{3,2,1,0:T(8,128)}, f32[6,8,8,512]{3,2,1,0:T(8,128)S(1)}, u32[]{:S(2)}) copy-start(f32[6,8,8,512]{3,2,1,0:T(8,128)S(1)} %bitcast_dynamic-update-slice_fusion.3) | copy-start | bytes 2359300
  93.1 0.7 copy-start.21
  93.1 0.7 copy-start.22
  93.1 0.7 copy-start.23
  100.6 7.7 %copy-start.4 = (f32[1,8,8,512]{3,2,1,0:T(8,128)S(1)}, f32[1,8,8,512]{3,2,1,0:T(8,128)}, u32[]{:S(2)}) copy-start(f32[1,8,8,512]{3,2,1,0:T(8,128)} %get-tuple-element.17) | copy-start | bytes 393220
  100.6 7.7 %copy-start.5 = (f32[1,8,8,512]{3,2,1,0:T(8,128)S(1)}, f32[1,8,8,512]{3,2,1,0:T(8,128)}, u32[]{:S(2)}) copy-start(f32[1,8,8,512]{3,2,1,0:T(8,128)} %get-tuple-element.33) | copy-start | bytes 393220
  100.6 7.7 %copy-start.6 = (f32[1,8,8,512]{3,2,1,0:T(8,128)S(1)}, f32[1,8,8,512]{3,2,1,0:T(8,128)}, u32[]{:S(2)}) copy-start(f32[1,8,8,512]{3,2,1,0:T(8,128)} %get-tuple-element.34) | copy-start | bytes 393220
  100.6 7.7 %copy-start.7 = (f32[1,8,8,512]{3,2,1,0:T(8,128)S(1)}, f32[1,8,8,512]{3,2,1,0:T(8,128)}, u32[]{:S(2)}) copy-start(f32[1,8,8,512]{3,2,1,0:T(8,128)} %get-tuple-element.35) | copy-start | bytes 393220
  100.7 7.7 %copy-start.8 = (f32[1,8,8,512]{3,2,1,0:T(8,128)S(1)}, f32[1,8,8,512]{3,2,1,0:T(8,128)}, u32[]{:S(2)}) copy-start(f32[1,8,8,512]{3,2,1,0:T(8,128)} %get-tuple-element.36) | copy-start | bytes 393220
  100.7 7.7 %copy-start.9 = (f32[1,8,8,512]{3,2,1,0:T(8,128)S(1)}, f32[1,8,8,512]{3,2,1,0:T(8,128)}, u32[]{:S(2)}) copy-start(f32[1,8,8,512]{3,2,1,0:T(8,128)} %get-tuple-element.37) | copy-start | bytes 393220
  100.7 7.7 %copy-start.10 = (f32[1,8,8,512]{3,2,1,0:T(8,128)S(1)}, f32[1,8,8,512]{3,2,1,0:T(8,128)}, u32[]{:S(2)}) copy-start(f32[1,8,8,512]{3,2,1,0:T(8,128)} %get-tuple-element.38) | copy-start | bytes 393220
  100.7 7.7 %copy-start.11 = (f32[1,8,8,512]{3,2,1,0:T(8,128)S(1)}, f32[1,8,8,512]{3,2,1,0:T(8,128)}, u32[]{:S(2)}) copy-start(f32[1,8,8,512]{3,2,1,0:T(8,128)} %get-tuple-element.39) | copy-start | bytes 393220
  102.0 12.8 %all-to-all-start = ((f32[6,32,128]{2,0,1:T(8,128)}), f32[6,32,128]{2,0,1:T(8,128)S(1)}, u32[]{:S(2)}, u32[]{:S(2)}) async-start(f32[6,32,128]{2,0,1:T(8,128)} %copy.65), calls=%async_computation | async-start | bytes 262144 | tf_op jit(solution)/shard_map/all_to_all | solution.py:145
  137.6 18.4 %all-to-all-start.1 = ((f32[3,32,128]{2,0,1:T(4,128)}), f32[3,32,128]{2,0,1:T(4,128)S(1)}, u32[]{:S(2)}, u32[]{:S(2)}) async-start(f32[3,32,128]{2,0,1:T(4,128)} %copy.68), calls=%async_computation.1 | async-start | bytes 131072 | tf_op jit(solution)/shard_map/all_to_all | solution.py:164
  273.3 10.6 %copy-start = (f32[3,2048]{0,1:T(8,128)S(1)}, f32[3,2048]{0,1:T(8,128)}, u32[]{:S(2)}) copy-start(f32[3,2048]{0,1:T(8,128)} %get-tuple-element.31) | copy-start | bytes 73732
  273.3 5.9 %collective-permute-start.2 = (f32[3,9,1,512]{3,2,1,0:T(1,128)S(1)}, f32[3,9,1,512]{3,2,1,0:T(1,128)S(1)}, u32[]{:S(2)}, u32[]{:S(2)}) collective-permute-start(f32[3,9,1,512]{3,2,1,0:T(1,128)S(1)} %slice.256), channel_id=1, source_target_pairs={{0,1},{1,2},{2,3},{3,4},{4,5},{5,6},{6,7},{8,9},{9,10},{10,11},{11... | collective-permute-start | bytes 165896 | tf_op jit(solution)/shard_map/ppermute | solution.py:13
  277.2 7.8 %copy-start.13 = (f32[8,8,512]{2,1,0:T(8,128)S(1)}, f32[8,8,512]{2,1,0:T(8,128)}, u32[]{:S(2)}) copy-start(f32[8,8,512]{2,1,0:T(8,128)} %param.18) | copy-start | bytes 393220
  279.3 5.7 %collective-permute-start.3 = (f32[3,1,8,512]{3,2,1,0:T(8,128)S(1)}, f32[3,1,8,512]{3,2,1,0:T(8,128)S(1)}, u32[]{:S(2)}, u32[]{:S(2)}) collective-permute-start(f32[3,1,8,512]{3,2,1,0:T(8,128)S(1)} %slice.258), channel_id=1, source_target_pairs={{0,8},{8,16},{16,24},{1,9},{9,17},{17,25},{2,10},{10,18},{18,26},{... | collective-permute-start | bytes 147464 | tf_op jit(solution)/shard_map/ppermute | solution.py:13
where the time goes:
time: 288 us; the launch traced here: 286 us
  other arithmetic  138 us (48%)
  local copies, waits for them, and re-layouts  117 us (41%)
  starting transfers between devices  24.8 us (9%)
  waiting for transfers between devices  5.52 us (2%)
    scatter-add x4, other arithmetic, per_device(): flat_forces = flat_forces.at[:, index].add(quarter)  98.5 us
    gather x7, local copies, waits for them, and re-layouts, per_device(): pieces.append(flat_disp[:, index] + shift_vec)  51.1 us
    ppermute x4, starting transfers between devices, shifted(): return lax.ppermute(array, axis, pairs)  13.3 us
    scatter-add x1, other arithmetic, per_device(): jnp.zeros((3, slots), jnp.float32).at[:, flat_candidates]  13.1 us
    reshape x2, local copies, waits for them, and re-layouts, per_device(): flat_forces = forces.reshape(3, -1)  12.5 us
    scatter-add x1, local copies, waits for them, and re-layouts, per_device(): flat_forces = flat_forces.at[:, index].add(quarter)  12 us
    reshape x2, local copies, waits for them, and re-layouts, per_device(): flat_disp = extended[3:6].reshape(3, -1)  11.3 us
    another operation x3, other arithmetic  9.41 us
  transfers between devices with their start and end apart: 6, of which 4 were waited for; matrix products, arithmetic and copies ran while one was open for 11% of the time, Pallas kernels for 0%

commit v1 on v0

v1 whole, which is shorter than its diff:
```python
import functools

import jax
import jax.numpy as jnp
from jax import lax
from jax.experimental import pallas as pl
from jax.experimental.pallas import tpu as pltpu
from jax.sharding import PartitionSpec as P

time_step = 0.1
penalty = 10.0
LANES = 128
F32 = jnp.float32
BF16 = jnp.bfloat16
VMEM = pl.BlockSpec(memory_space=pltpu.VMEM)
NN = (((1,), (0,)), ((), ()))
NT = (((1,), (1,)), ((), ()))


def split_index(value, size):
    if size & (size - 1) == 0:
        return value >> (size.bit_length() - 1), value & (size - 1)
    return value // size, value % size


def two_terms(value):
    high = value.astype(BF16)
    return high, (value - high.astype(F32)).astype(BF16)


def dot(left, right, dims):
    return lax.dot_general(left, right, dims, preferred_element_type=F32)


def one_hot(row, count):
    return lax.broadcasted_iota(jnp.int32, (count, row.shape[1]), 0) == row


def next_row(tile, last):
    rows = tile.shape[0]
    rolled = pltpu.roll(tile, rows - 1, 0)
    return jnp.where(lax.broadcasted_iota(jnp.int32, tile.shape, 0) == rows - 1, last, rolled)


def previous_row(tile):
    rolled = pltpu.roll(tile, 1, 0)
    return jnp.where(lax.broadcasted_iota(jnp.int32, tile.shape, 0) == 0, 0.0, rolled)


def next_lane(tile):
    lanes = tile.shape[1]
    rolled = pltpu.roll(tile, lanes - 1, 1)
    return jnp.where(lax.broadcasted_iota(jnp.int32, tile.shape, 1) == lanes - 1, 0.0, rolled)


def previous_lane(tile):
    rolled = pltpu.roll(tile, 1, 1)
    return jnp.where(lax.broadcasted_iota(jnp.int32, tile.shape, 1) == 0, 0.0, rolled)


def index_kernel(devices, capacity, size_z, elem, bucket, out):
    count = elem.shape[1]
    row, depth = split_index(elem[...], size_z)
    out[0:1] = depth + 1
    out[1:2] = row
    tri = (
        lax.broadcasted_iota(jnp.int32, (LANES, LANES), 0)
        <= lax.broadcasted_iota(jnp.int32, (LANES, LANES), 1)
    ).astype(F32).astype(BF16)
    carry = jnp.zeros((devices, 1), F32)
    for start in range(0, count, LANES):
        here = bucket[:, start : start + LANES]
        hot = one_hot(here, devices).astype(F32)
        running = dot(hot.astype(BF16), tri, NN)
        rank = jnp.sum(hot * (running + carry), axis=0, keepdims=True) - 1.0
        carry = carry + running[:, LANES - 1 : LANES]
        target = here * capacity + rank.astype(jnp.int32)
        high, low = split_index(target, LANES)
        out[2:3, start : start + LANES] = high
        out[3:4, start : start + LANES] = low
    out[4:8] = jnp.zeros((4, count), jnp.int32)


def spread(values, high, groups):
    rows, lanes = values.shape
    which = lax.broadcasted_iota(jnp.int32, (groups, rows, lanes), 0)
    kept = jnp.where(which == high[None], values[None], 0.0)
    return kept.reshape(groups * rows, lanes)


def picked(table, high, groups):
    rows = table.shape[0] // groups
    lanes = table.shape[1]
    total = jnp.zeros((rows, lanes), F32)
    for group in range(groups):
        total = jnp.where(high == group, table[group * rows : (group + 1) * rows], total)
    return total


def geometry_kernel(chunk, own, ghost_x, ghost_y, ghost_c, index, out, faces, payload):
    size_x, size_y, size_z = own.shape[1:]
    groups = out.shape[0]
    count = index.shape[1]

    def plane(comp, i):
        return own[comp, i] if i < size_x else ghost_x[comp]

    def last_row(comp, i):
        return ghost_y[comp, i : i + 1] if i < size_x else ghost_c[comp : comp + 1]

    for i in range(size_x):
        p, q = [], []
        for comp in range(3):
            low, high = plane(comp, i), plane(comp, i + 1)
            low_next = next_row(low, last_row(comp, i))
            high_next = next_row(high, last_row(comp, i + 1))
            faces[comp, i] = 0.25 * ((low + high) + (low_next + high_next))
            p.append(high_next - low)
            q.append(low_next - high)
        faces[3, i] = 0.5 * ((1.0 + p[1]) * q[2] - p[2] * (1.0 + q[1]))
        faces[4, i] = 0.5 * (p[2] * (q[0] - 1.0) - (1.0 + p[0]) * q[2])
        faces[5, i] = 0.5 * (p[0] + p[1] + q[1] - q[0] + p[0] * q[1] - p[1] * q[0])
    rows = size_x * size_y
    high, low = two_terms(faces[...].reshape(6 * rows, size_z))
    total = jnp.zeros((groups * 8, LANES), F32)
    payload[6:7] = jnp.ones((1, chunk), F32)
    payload[7:8] = jnp.zeros((1, chunk), F32)
    for start in range(0, count, chunk):
        here = slice(start, start + chunk)
        hot = one_hot(index[0:1, here], size_z).astype(F32).astype(BF16)
        near = dot(high, hot, NN) + dot(low, hot, NN)
        hot_row = one_hot(index[1:2, here], rows)
        for comp in range(6):
            payload[comp : comp + 1] = jnp.sum(
                jnp.where(hot_row, near[comp * rows : (comp + 1) * rows], 0.0), axis=0, keepdims=True
            )
        slot = index[2:3, here]
        hot_low = one_hot(index[3:4, here], LANES).astype(F32).astype(BF16)
        values = payload[...]
        part = values.astype(BF16).astype(F32)
        total += dot(spread(part, slot, groups).astype(BF16), hot_low, NT)
        total += dot(spread(values - part, slot, groups).astype(BF16), hot_low, NT)
    out[...] = total.reshape(out.shape)


def stress_kernel(
    own, ghost_x, ghost_y, ghost_c, stress, lame_lambda, lame_mu,
    new_stress, force, force_x, force_y, force_c,
):
    size_x = own.shape[1]
    size_y = own.shape[2]

    def plane(comp, i):
        tile = own[comp, i] if i < size_x else ghost_x[comp]
        last = ghost_y[comp, i : i + 1] if i < size_x else ghost_c[comp : comp + 1]
        after = next_row(tile, last)
        both, change = tile + after, after - tile
        return both + next_lane(both), change + next_lane(change), next_lane(both) - both

    low = [plane(comp, 0) for comp in range(3)]
    carry = None
    for i in range(size_x):
        high = [plane(comp, i + 1) for comp in range(3)]
        grad_x = [high[c][0] - low[c][0] for c in range(3)]
        grad_y = [high[c][1] + low[c][1] for c in range(3)]
        grad_z = [high[c][2] + low[c][2] for c in range(3)]
        low = high
        shear = (0.5 * time_step) * lame_mu[i]
        volume = (0.25 * time_step) * lame_lambda[i] * (grad_x[0] + grad_y[1] + grad_z[2])
        s_xx = stress[0, i] + (volume + shear * grad_x[0])
        s_yy = stress[1, i] + (volume + shear * grad_y[1])
        s_zz = stress[2, i] + (volume + shear * grad_z[2])
        half = 0.5 * shear
        s_yz = stress[3, i] + half * (grad_z[1] + grad_y[2])
        s_xz = stress[4, i] + half * (grad_z[0] + grad_x[2])
        s_xy = stress[5, i] + half * (grad_y[0] + grad_x[1])
        for number, value in enumerate((s_xx, s_yy, s_zz, s_yz, s_xz, s_xy)):
            new_stress[number, i] = value
        tensor = ((s_xx, s_xy, s_xz), (s_xy, s_yy, s_yz), (s_xz, s_yz, s_zz))
        later = []
        for comp in range(3):
            first, second, third = (-0.25 * t for t in tensor[comp])
            first = first + previous_lane(first)
            second = second + previous_lane(second)
            third = previous_lane(third) - third
            near_plus, near_minus = third - second + first, third - second - first
            far_plus, far_minus = third + second + first, third + second - first
            plus = near_plus + previous_row(far_plus)
            minus = near_minus + previous_row(far_minus)
            plus_end = far_plus[size_y - 1 : size_y]
            minus_end = far_minus[size_y - 1 : size_y]
            if carry is not None:
                minus = minus + carry[comp][0]
                minus_end = minus_end + carry[comp][1]
            force[comp, i] = minus
            force_y[comp, i : i + 1] = minus_end
            later.append((plus, plus_end))
        carry = later
    for comp in range(3):
        force_x[comp] = carry[comp][0]
        force_c[comp : comp + 1] = carry[comp][1]


def contact_kernel(arrived, points, candidates, slave_force, reaction):
    groups = arrived.shape[0]
    lanes = points.shape[1]
    high, low = two_terms(arrived[...].reshape(groups * 8, LANES))
    total = jnp.zeros((groups * 8, LANES), F32)
    pushed = [jnp.zeros((1, lanes), F32) for _ in range(3)]
    eight = lax.broadcasted_iota(jnp.int32, (8, lanes), 0)
    for k in range(candidates.shape[0]):
        slot, place = split_index(candidates[k : k + 1], LANES)
        hot = one_hot(place, LANES).astype(F32).astype(BF16)
        near = picked(dot(high, hot, NN) + dot(low, hot, NN), slot, groups)
        rows = [near[r : r + 1] for r in range(7)]
        filled = rows[6]
        offset = (0.5, 0.5, 1.0)
        area = (rows[3], rows[4], rows[5] + filled)
        gap = jnp.zeros((1, lanes), F32)
        for comp in range(3):
            gap = gap + area[comp] * (points[comp : comp + 1] - (rows[comp] + offset[comp] * filled))
        scale = penalty * jnp.maximum(-gap, 0.0)
        values = jnp.zeros((8, lanes), F32)
        for comp in range(3):
            push = scale * area[comp]
            pushed[comp] = pushed[comp] + push
            values = jnp.where(eight == comp, -push, values)
        part = values.astype(BF16).astype(F32)
        total += dot(spread(part, slot, groups).astype(BF16), hot, NT)
        total += dot(spread(values - part, slot, groups).astype(BF16), hot, NT)
    for comp in range(3):
        slave_force[comp : comp + 1] = pushed[comp]
    reaction[...] = total.reshape(reaction.shape)


def nodes_kernel(
    chunk, returned, index, in_force, in_x, in_y, in_c, force, force_x, force_y, force_c
):
    size_x, size_y, size_z = in_force.shape[1:]
    groups = returned.shape[0]
    count = index.shape[1]
    rows = size_x * size_y
    high, low = two_terms(returned[...].reshape(groups * 8, LANES))
    total = jnp.zeros((3 * rows, size_z), F32)
    for start in range(0, count, chunk):
        here = slice(start, start + chunk)
        hot_low = one_hot(index[3:4, here], LANES).astype(F32).astype(BF16)
        near = picked(dot(high, hot_low, NN) + dot(low, hot_low, NN), index[2:3, here], groups)
        quarter = 0.25 * near
        part = quarter.astype(BF16).astype(F32)
        rest = quarter - part
        hot_row = one_hot(index[1:2, here], rows)
        hot = one_hot(index[0:1, here], size_z).astype(F32).astype(BF16)
        for values in (part, rest):
            left = jnp.concatenate(
                [jnp.where(hot_row, values[c : c + 1], 0.0) for c in range(3)], 0
            ).astype(BF16)
            total += dot(left, hot, NT)
    for comp in range(3):
        before = None
        for i in range(size_x):
            at = (comp * size_x + i) * size_y
            tile = total[at : at + size_y]
            both = tile + previous_row(tile)
            end = tile[size_y - 1 : size_y]
            value, value_end = both, end
            if before is not None:
                value, value_end = both + before[0], end + before[1]
            force[comp, i] = in_force[comp, i] + value
            force_y[comp, i : i + 1] = in_y[comp, i : i + 1] + value_end
            before = (both, end)
        force_x[comp] = in_x[comp] + before[0]
        force_c[comp : comp + 1] = in_c[comp : comp + 1] + before[1]


def final_kernel(force, from_x, from_y, from_c, mass, out):
    size_x = force.shape[1]
    first = lax.broadcasted_iota(jnp.int32, force.shape[2:], 0) == 0
    for i in range(size_x):
        inverse = 1.0 / mass[i]
        for comp in range(3):
            end = from_y[comp, i : i + 1]
            value = force[comp, i]
            if i == 0:
                end = end + from_c[comp : comp + 1]
                value = value + from_x[comp]
            out[comp, i] = (value + jnp.where(first, end, 0.0)) * inverse


def call(kernel, outs, *args, scratch=(), flops=0):
    moved = sum(a.size * 4 for a in args) + sum(4 * functools.reduce(lambda x, y: x * y, s) for s, _ in outs)
    return pl.pallas_call(
        kernel,
        out_shape=[jax.ShapeDtypeStruct(s, d) for s, d in outs],
        in_specs=[VMEM] * len(args),
        out_specs=[VMEM] * len(outs),
        scratch_shapes=list(scratch),
        compiler_params=pltpu.CompilerParams(vmem_limit_bytes=48 * 1024 * 1024),
        cost_estimate=pl.CostEstimate(flops=flops, bytes_accessed=moved, transcendentals=0),
    )(*args)


def moves(count_x, count_y, by_x, by_y):
    pairs = []
    for x in range(count_x):
        for y in range(count_y):
            to_x, to_y = x + by_x, y + by_y
            if 0 <= to_x < count_x and 0 <= to_y < count_y:
                pairs.append((x * count_y + y, to_x * count_y + to_y))
    return pairs


def exchange(slots, devices):
    groups, rows, lanes = slots.shape
    per = devices // groups
    if per > 1:
        slots = slots.reshape(groups, rows, per, lanes // per).transpose(0, 2, 1, 3)
        slots = slots.reshape(devices, rows, lanes // per)
    slots = lax.all_to_all(slots, ("gx", "gy"), split_axis=0, concat_axis=0, tiled=True)
    if per > 1:
        slots = slots.reshape(groups, per, rows, lanes // per).transpose(0, 2, 1, 3)
        slots = slots.reshape(groups, rows, lanes)
    return slots


def per_device(
    velocity, stress, lame_lambda, lame_mu, node_mass, displacement,
    seg_elem, seg_bucket, slave_points, candidates,
):
    count_x = lax.axis_size("gx")
    count_y = lax.axis_size("gy")
    devices = count_x * count_y
    _, size_x, size_y, size_z = velocity.shape
    seg_count = seg_elem.shape[0]
    capacity = 2 * seg_count // devices
    slots = devices * capacity
    groups = slots // LANES
    axes = ("gx", "gy")

    def ghosts(own):
        return (
            lax.ppermute(own[:, 0], axes, moves(count_x, count_y, -1, 0)),
            lax.ppermute(own[:, :, 0], axes, moves(count_x, count_y, 0, -1)),
            lax.ppermute(own[:, 0, 0], axes, moves(count_x, count_y, -1, -1)),
        )

    disp_ghosts = ghosts(displacement)
    vel_ghosts = ghosts(velocity)
    (index,) = call(
        functools.partial(index_kernel, devices, capacity, size_z),
        [((8, seg_count), jnp.int32)],
        seg_elem.reshape(1, seg_count),
        seg_bucket.reshape(1, seg_count),
        flops=4_000_000_000,
    )
    chunk = min(512, seg_count)
    (outgoing,) = call(
        functools.partial(geometry_kernel, chunk),
        [((groups, 8, LANES), F32)],
        displacement, *disp_ghosts, index,
        scratch=[pltpu.VMEM((6, size_x, size_y, size_z), F32), pltpu.VMEM((8, chunk), F32)],
        flops=4_000_000_000,
    )
    arrived = exchange(outgoing, devices)
    plane = (3, size_y, size_z)
    planes = [
        (velocity.shape, F32), (plane, F32), ((3, size_x, size_z), F32), ((3, size_z), F32)
    ]
    new_stress, *forces = call(
        stress_kernel,
        [(stress.shape, F32)] + planes,
        velocity, *vel_ghosts, stress, lame_lambda, lame_mu,
        flops=8_000_000_000,
    )
    slave_force, reaction = call(
        contact_kernel,
        [(slave_points.shape, F32), ((groups, 8, LANES), F32)],
        arrived, slave_points, candidates,
        flops=2_000_000_000,
    )
    returned = exchange(reaction, devices)
    force, force_x, force_y, force_c = call(
        functools.partial(nodes_kernel, chunk), planes, returned, index, *forces,
        flops=4_000_000_000,
    )
    from_x = lax.ppermute(force_x, axes, moves(count_x, count_y, 1, 0))
    from_y = lax.ppermute(force_y, axes, moves(count_x, count_y, 0, 1))
    from_c = lax.ppermute(force_c, axes, moves(count_x, count_y, 1, 1))
    (acceleration,) = call(
        final_kernel, [(velocity.shape, F32)], force, from_x, from_y, from_c, node_mass
    )
    return (new_stress, acceleration, slave_force)


def solution(mesh):
    grid = P(None, "gx", "gy", None)
    cells = P("gx", "gy", None)
    return jax.shard_map(
        per_device,
        mesh=mesh,
        in_specs=(
            grid, grid, cells, cells, cells, grid,
            P(("gx", "gy")), P(("gx", "gy"), None), P(None, ("gx", "gy")), P(None, ("gx", "gy")),
        ),
        out_specs=(grid, grid, P(None, ("gx", "gy"))),
        check_vma=False,
    )
```

time: 288 us -> 62.6 us (0.22)
  other arithmetic: 138 us -> 0 us
  local copies, waits for them, and re-layouts: 117 us -> 1.71 us
  Pallas kernels: 0 us -> 12.4 us
  starting transfers between devices: 24.8 us -> 36.7 us
  waiting for transfers between devices: 5.52 us -> 9.73 us
    scatter-add x5 -> x0, other arithmetic: 112 us -> none  [the longest x4 98.5 us: per_device(): flat_forces = flat_forces.at[:, index].add(quarter)]
    gather x9 -> x0, local copies, waits for them, and re-layouts: 62 us -> none  [the longest x7 51.1 us: per_device(): pieces.append(flat_disp[:, index] + shift_vec)]
    reshape x7 -> x0, local copies, waits for them, and re-layouts: 27 us -> none  [the longest x2 12.5 us: per_device(): flat_forces = forces.reshape(3, -1)]
    another operation x7 -> x0, other arithmetic: 14.6 us -> none
    pallas_call x0 -> x6, Pallas kernels: none -> 12.4 us  [call(): pl.pallas_call(kernel, out_shape=[jax.ShapeDtypeStruct(s, d) for s, d in...]
    scatter-add x1 -> x0, local copies, waits for them, and re-layouts: 12 us -> none  [per_device(): flat_forces = flat_forces.at[:, index].add(quarter)]
    ppermute x4 -> x9, starting transfers between devices: 13.3 us -> 23.6 us  [the longest x2 6.89 us: ghosts(): lax.ppermute(own[:, 0, 0], axes, moves(count_x, count_y, -1, -1))]
    scatter x1 -> x0, local copies, waits for them, and re-layouts: 6.22 us -> none  [per_device(): outgoing = jnp.zeros((width, slots), jnp.float32).at[:, target].set(payload)]
  transfers between devices with their start and end apart: 6 -> 11, of which waited for: 4 -> 4; matrix products, arithmetic and copies ran while one was open for 11% -> 1% of each run, Pallas kernels for 0% -> 8%
where the time goes in v1:
time: 62.6 us; the launch traced here: 61.5 us
  starting transfers between devices  36.7 us (59%)
  Pallas kernels  12.4 us (20%)
  waiting for transfers between devices  9.73 us (16%)
  local copies, waits for them, and re-layouts  1.71 us (3%)
  between operations  0.97 us (2%)
    all_to_all x2, starting transfers between devices, exchange(): lax.all_to_all(slots, ('gx', 'gy'), split_axis=0, concat_axis=0, tiled=True)  13.1 us
    pallas_call x6, Pallas kernels, call(): pl.pallas_call(kernel, out_shape=[jax.ShapeDtypeStruct(s, d) for s, d in...  12.4 us
    ppermute x2, starting transfers between devices, ghosts(): lax.ppermute(own[:, 0, 0], axes, moves(count_x, count_y, -1, -1))  6.89 us
    all_to_all x2, waiting for transfers between devices, exchange(): lax.all_to_all(slots, ('gx', 'gy'), split_axis=0, concat_axis=0, tiled=True)  4.59 us
    ppermute x2, starting transfers between devices, ghosts(): lax.ppermute(own[:, 0], axes, moves(count_x, count_y, -1, 0))  4.09 us
    ppermute x2, starting transfers between devices, ghosts(): lax.ppermute(own[:, :, 0], axes, moves(count_x, count_y, 0, -1))  3.97 us
    ppermute x1, starting transfers between devices, per_device(): from_c = lax.ppermute(force_c, axes, moves(count_x, count_y, 1, 1))  3.24 us
    ppermute x1, starting transfers between devices, per_device(): from_x = lax.ppermute(force_x, axes, moves(count_x, count_y, 1, 0))  2.88 us
  transfers between devices with their start and end apart: 11, of which 4 were waited for; matrix products, arithmetic and copies ran while one was open for 1% of the time, Pallas kernels for 8%

profile of v1, /device:TPU:9, one launch (start us, length us, event | category | flops | bytes accessed | tf_op | source)
XLA Modules:
  0.0 61.5 jit_solution(5091280196977442187)
XLA Ops:
  0.6 0.8 %slice.23 = f32[3,1,1,512]{3,2,1,0:T(1,128)S(1)} slice(f32[3,8,8,512]{3,2,1,0:T(8,128)} %own.3), slice={[0:3], [0:1], [0:1], [0:512]} | slice | bytes 12288 | tf_op jit(solution)/shard_map/slice | solution.py:344
  1.4 3.6 %collective-permute-start.5 = (f32[3,512]{1,0:T(4,128)S(1)}, f32[3,512]{1,0:T(4,128)S(1)}, u32[]{:S(2)}, u32[]{:S(2)}) collective-permute-start(f32[3,512]{1,0:T(4,128)S(1)} %bitcast.27), channel_id=1, source_target_pairs={{9,0},{10,1},{11,2},{12,3},{13,4},{14,5},{15,6},{17,8},{18,9},{19,... | collective-permute-start | bytes 18440 | tf_op jit(solution)/shard_map/ppermute | solution.py:344
  5.0 0.8 %slice_bitcast_fusion = f32[3,8,512]{2,1,0:T(8,128)S(1)} fusion(f32[3,8,8,512]{3,2,1,0:T(8,128)} %own.3), kind=kLoop, calls=%fused_computation.2 | loop fusion | bytes 98304 | tf_op jit(solution)/shard_map/squeeze | solution.py:342
  5.8 2.0 %collective-permute-start.3 = (f32[3,8,512]{2,1,0:T(8,128)S(1)}, f32[3,8,512]{2,1,0:T(8,128)S(1)}, u32[]{:S(2)}, u32[]{:S(2)}) collective-permute-start(f32[3,8,512]{2,1,0:T(8,128)S(1)} %slice_bitcast_fusion), channel_id=1, source_target_pairs={{8,0},{9,1},{10,2},{11,3},{12,4},{13,5},{14,6},{15,7},{16,8},{17,9... | collective-permute-start | bytes 147464 | tf_op jit(solution)/shard_map/ppermute | solution.py:342
  7.9 0.0 slice-done
  7.9 0.0 copy-start.6
  7.9 0.0 copy-start.7
  7.9 1.9 %collective-permute-start.4 = (f32[3,8,512]{2,1,0:T(8,128)S(1)}, f32[3,8,512]{2,1,0:T(8,128)S(1)}, u32[]{:S(2)}, u32[]{:S(2)}) collective-permute-start(f32[3,8,512]{2,1,0:T(8,128)S(1)} %bitcast.25), channel_id=1, source_target_pairs={{1,0},{2,1},{3,2},{4,3},{5,4},{6,5},{7,6},{9,8},{10,9},{11,10},{12... | collective-permute-start | bytes 147464 | tf_op jit(solution)/shard_map/ppermute | solution.py:343
  9.8 0.0 copy-done.6
  9.8 0.0 copy-done.7
  9.9 0.0 copy-start.1
  9.9 0.3 shard_map.122.index
  10.2 0.0 copy-start.2
  10.2 0.0 collective-permute-done.5.ghost_c
  10.2 1.1 %collective-permute-done.3.ghost_x = f32[3,8,512]{2,1,0:T(8,128)S(1)} collective-permute-done((f32[3,8,512]{2,1,0:T(8,128)S(1)}, f32[3,8,512]{2,1,0:T(8,128)S(1)}, u32[]{:S(2)}, u32[]{:S(2)}) %collective-permute-start.3) | collective-permute-done | bytes 49184 | tf_op jit(solution)/shard_map/ppermute | solution.py:342
  11.3 1.4 %collective-permute-done.4.ghost_y = f32[3,8,512]{2,1,0:T(8,128)S(1)} collective-permute-done((f32[3,8,512]{2,1,0:T(8,128)S(1)}, f32[3,8,512]{2,1,0:T(8,128)S(1)}, u32[]{:S(2)}, u32[]{:S(2)}) %collective-permute-start.4) | collective-permute-done | bytes 49184 | tf_op jit(solution)/shard_map/ppermute | solution.py:343
  12.7 0.0 copy-done.1
  12.7 4.3 %shard_map.123 = f32[32,8,128]{2,1,0:T(8,128)} custom-call(f32[3,8,8,512]{3,2,1,0:T(8,128)S(1)} %copy-done.1, f32[3,8,512]{2,1,0:T(8,128)S(1)} %collective-permute-done.3.ghost_x, f32[3,8,512]{2,1,0:T(8,128)S(1)} %collective-permute-done.4.ghost_y, f32[3,512]{1,0:T(4,128)S(1)} %collective-permute-done.5.ghost_c, s32[8,2048]{1,0:T(8,128)S(1)} %shard_map.122.index), custom_call_target="tpu_custom_call" | custom-call | flops 4000000000 | bytes 694272 | tf_op jit(solution)/shard_map/pallas_call | solution.py:292
  17.1 6.5 %all-to-all-start = ((f32[32,8,128]{2,1,0:T(8,128)}), f32[32,8,128]{2,1,0:T(8,128)S(1)}, u32[]{:S(2)}, u32[]{:S(2)}) async-start(f32[32,8,128]{2,1,0:T(8,128)} %shard_map.123), calls=%async_computation | async-start | bytes 262144 | tf_op jit(solution)/shard_map/all_to_all | solution.py:319
  23.6 0.0 copy-done.2
  23.6 3.3 %collective-permute-start.2 = (f32[3,512]{1,0:T(4,128)S(1)}, f32[3,512]{1,0:T(4,128)S(1)}, u32[]{:S(2)}, u32[]{:S(2)}) collective-permute-start(f32[3,512]{1,0:T(4,128)S(1)} %bitcast.26), channel_id=1, source_target_pairs={{9,0},{10,1},{11,2},{12,3},{13,4},{14,5},{15,6},{17,8},{18,9},{19,... | collective-permute-start | bytes 18440 | tf_op jit(solution)/shard_map/ppermute | solution.py:344
  27.0 0.0 slice-start.1
  27.0 2.1 %collective-permute-start = (f32[3,8,512]{2,1,0:T(8,128)S(1)}, f32[3,8,512]{2,1,0:T(8,128)S(1)}, u32[]{:S(2)}, u32[]{:S(2)}) collective-permute-start(f32[3,8,512]{2,1,0:T(8,128)S(1)} %slice_bitcast_fusion.1), channel_id=1, source_target_pairs={{8,0},{9,1},{10,2},{11,3},{12,4},{13,5},{14,6},{15,7},{16,8},{17,9... | collective-permute-start | bytes 147464 | tf_op jit(solution)/shard_map/ppermute | solution.py:342
  29.1 0.0 slice-done.1
  29.1 0.0 copy-start.8
  29.1 0.0 copy-start.9
  29.1 0.0 copy-start.3
  29.1 2.1 %collective-permute-start.1 = (f32[3,8,512]{2,1,0:T(8,128)S(1)}, f32[3,8,512]{2,1,0:T(8,128)S(1)}, u32[]{:S(2)}, u32[]{:S(2)}) collective-permute-start(f32[3,8,512]{2,1,0:T(8,128)S(1)} %bitcast.24), channel_id=1, source_target_pairs={{1,0},{2,1},{3,2},{4,3},{5,4},{6,5},{7,6},{9,8},{10,9},{11,10},{12... | collective-permute-start | bytes 147464 | tf_op jit(solution)/shard_map/ppermute | solution.py:343
  31.2 0.0 all-to-all-done.arrived
  31.2 0.0 copy-done.8
  31.2 2.5 %shard_map.124 = (f32[3,512]{1,0:T(4,128)}, f32[32,8,128]{2,1,0:T(8,128)}) custom-call(f32[32,8,128]{2,1,0:T(8,128)S(1)} %all-to-all-done.arrived, f32[3,512]{1,0:T(4,128)S(1)} %copy-done.8, s32[4,512]{1,0:T(4,128)S(1)} %copy-done.9), custom_call_target="tpu_custom_call" | custom-call | flops 2000000000 | bytes 282624 | tf_op jit(solution)/shard_map/pallas_call | solution.py:292
  33.7 6.6 %all-to-all-start.1 = ((f32[32,8,128]{2,1,0:T(8,128)}), f32[32,8,128]{2,1,0:T(8,128)S(1)}, u32[]{:S(2)}, u32[]{:S(2)}) async-start(f32[32,8,128]{2,1,0:T(8,128)} %get-tuple-element.15), calls=%async_computation.1 | async-start | bytes 262144 | tf_op jit(solution)/shard_map/all_to_all | solution.py:319
  40.3 0.0 collective-permute-done.2.ghost_c
  40.3 0.0 collective-permute-done.ghost_x
  40.3 0.0 collective-permute-done.1.ghost_y
  40.3 0.0 copy-done.3
  40.4 0.0 copy-done.4
  40.4 0.0 copy-done.5
  40.4 1.9 %shard_map.121 = (f32[6,8,8,512]{3,2,1,0:T(8,128)}, f32[3,8,8,512]{3,2,1,0:T(8,128)S(1)}, f32[3,8,512]{2,1,0:T(8,128)S(1)}, f32[3,8,512]{2,1,0:T(8,128)S(1)}, f32[3,512]{1,0:T(4,128)S(1)}) custom-call(f32[3,8,8,512]{3,2,1,0:T(8,128)S(1)} %copy-done.2, f32[3,8,512]{2,1,0:T(8,128)S(1)} %collective-permute-done.ghost_x, ...), custom_call_target="tpu_custom_call" | custom-call | flops 8000000000 | bytes 2830336 | tf_op jit(solution)/shard_map/pallas_call | solution.py:292
  42.2 4.6 %all-to-all-done.1.returned = f32[32,8,128]{2,1,0:T(8,128)S(1)} async-done(((f32[32,8,128]{2,1,0:T(8,128)}), f32[32,8,128]{2,1,0:T(8,128)S(1)}, u32[]{:S(2)}, u32[]{:S(2)}) %all-to-all-start.1) | async-done | bytes 131104 | tf_op jit(solution)/shard_map/all_to_all | solution.py:319
  46.8 2.6 %shard_map.125 = (f32[3,8,8,512]{3,2,1,0:T(8,128)S(1)}, f32[3,8,512]{2,1,0:T(8,128)S(1)}, f32[3,8,512]{2,1,0:T(8,128)S(1)}, f32[3,512]{1,0:T(4,128)S(1)}) custom-call(f32[32,8,128]{2,1,0:T(8,128)S(1)} %all-to-all-done.1.returned, s32[8,2048]{1,0:T(8,128)S(1)} %shard_map.122.index, f32[3,8,8,512]{3,2,1,0:T(8,128)S(1)} %get-tuple-element.16.in_force, ...), custom_call_target="tpu_custom_call" | custom-call | flops 4000000000 | bytes 1191936 | tf_op jit(solution)/shard_map/pallas_call | solution.py:292
  49.4 2.9 %collective-permute-start.6 = (f32[3,8,512]{2,1,0:T(8,128)S(1)}, f32[3,8,512]{2,1,0:T(8,128)S(1)}, u32[]{:S(2)}, u32[]{:S(2)}) collective-permute-start(f32[3,8,512]{2,1,0:T(8,128)S(1)} %get-tuple-element.21), channel_id=1, source_target_pairs={{0,8},{1,9},{2,10},{3,11},{4,12},{5,13},{6,14},{7,15},{8,16},{9,17... | collective-permute-start | bytes 147464 | tf_op jit(solution)/shard_map/ppermute | solution.py:386
  52.3 2.5 %collective-permute-start.7 = (f32[3,8,512]{2,1,0:T(8,128)S(1)}, f32[3,8,512]{2,1,0:T(8,128)S(1)}, u32[]{:S(2)}, u32[]{:S(2)}) collective-permute-start(f32[3,8,512]{2,1,0:T(8,128)S(1)} %get-tuple-element.22), channel_id=1, source_target_pairs={{0,1},{1,2},{2,3},{3,4},{4,5},{5,6},{6,7},{8,9},{9,10},{10,11},{11... | collective-permute-start | bytes 147464 | tf_op jit(solution)/shard_map/ppermute | solution.py:387
  54.8 3.2 %collective-permute-start.8 = (f32[3,512]{1,0:T(4,128)S(1)}, f32[3,512]{1,0:T(4,128)S(1)}, u32[]{:S(2)}, u32[]{:S(2)}) collective-permute-start(f32[3,512]{1,0:T(4,128)S(1)} %get-tuple-element.23), channel_id=1, source_target_pairs={{0,9},{1,10},{2,11},{3,12},{4,13},{5,14},{6,15},{8,17},{9,18},{10,... | collective-permute-start | bytes 18440 | tf_op jit(solution)/shard_map/ppermute | solution.py:388
  58.1 2.6 %collective-permute-done.8.from_c = f32[3,512]{1,0:T(4,128)S(1)} collective-permute-done((f32[3,512]{1,0:T(4,128)S(1)}, f32[3,512]{1,0:T(4,128)S(1)}, u32[]{:S(2)}, u32[]{:S(2)}) %collective-permute-start.8) | collective-permute-done | bytes 6176 | tf_op jit(solution)/shard_map/ppermute | solution.py:388
  60.7 0.0 collective-permute-done.6.from_x
  60.7 0.0 collective-permute-done.7.from_y
  60.7 0.8 %shard_map.126 = f32[3,8,8,512]{3,2,1,0:T(8,128)} custom-call(f32[3,8,8,512]{3,2,1,0:T(8,128)S(1)} %get-tuple-element.20.force, f32[3,8,512]{2,1,0:T(8,128)S(1)} %collective-permute-done.6.from_x, f32[3,8,512]{2,1,0:T(8,128)S(1)} %collective-permute-done.7.from_y, f32[3,512]{1,0:T(4,128)S(1)} %collective-permute-done.8.from_c, f32[8,8,512]{2,1,0:T(8,128)S(1)} %copy-done), custom_call_target="tpu_custom_call" | custom-call | bytes 1021952 | tf_op jit(solution)/shard_map/pallas_call | solution.py:292
  (12 shorter events, 0.0 us)
Async XLA Ops:
  1.4 8.8 %collective-permute-start.5 = (f32[3,512]{1,0:T(4,128)S(1)}, f32[3,512]{1,0:T(4,128)S(1)}, u32[]{:S(2)}, u32[]{:S(2)}) collective-permute-start(f32[3,512]{1,0:T(4,128)S(1)} %bitcast.27), channel_id=1, source_target_pairs={{9,0},{10,1},{11,2},{12,3},{13,4},{14,5},{15,6},{17,8},{18,9},{19,... | collective-permute-start | bytes 18440 | tf_op jit(solution)/shard_map/ppermute | solution.py:344
  5.8 2.1 %slice-start = ((f32[3,8,8,512]{3,2,1,0:T(8,128)}), f32[3,8,1,512]{3,2,1,0:T(1,128)S(1)}, s32[]{:S(2)}) async-start(f32[3,8,8,512]{3,2,1,0:T(8,128)} %own.3), calls=%async_computation.2 | async-start | bytes 98304 | tf_op jit(solution)/shard_map/slice | solution.py:343
  5.8 5.5 %collective-permute-start.3 = (f32[3,8,512]{2,1,0:T(8,128)S(1)}, f32[3,8,512]{2,1,0:T(8,128)S(1)}, u32[]{:S(2)}, u32[]{:S(2)}) collective-permute-start(f32[3,8,512]{2,1,0:T(8,128)S(1)} %slice_bitcast_fusion), channel_id=1, source_target_pairs={{8,0},{9,1},{10,2},{11,3},{12,4},{13,5},{14,6},{15,7},{16,8},{17,9... | collective-permute-start | bytes 147464 | tf_op jit(solution)/shard_map/ppermute | solution.py:342
  7.9 2.0 %copy-start.6 = (s32[2048]{0:T(1024)S(1)}, s32[2048]{0:T(1024)}, u32[]{:S(2)}) copy-start(s32[2048]{0:T(1024)} %param.16) | copy-start | bytes 24580
  7.9 2.0 %copy-start.7 = (s32[2048,1]{0,1:T(1,128)S(1)}, s32[2048,1]{0,1:T(1,128)}, u32[]{:S(2)}) copy-start(s32[2048,1]{0,1:T(1,128)} %param.17) | copy-start | bytes 24580
  7.9 4.8 %collective-permute-start.4 = (f32[3,8,512]{2,1,0:T(8,128)S(1)}, f32[3,8,512]{2,1,0:T(8,128)S(1)}, u32[]{:S(2)}, u32[]{:S(2)}) collective-permute-start(f32[3,8,512]{2,1,0:T(8,128)S(1)} %bitcast.25), channel_id=1, source_target_pairs={{1,0},{2,1},{3,2},{4,3},{5,4},{6,5},{7,6},{9,8},{10,9},{11,10},{12... | collective-permute-start | bytes 147464 | tf_op jit(solution)/shard_map/ppermute | solution.py:343
  9.9 2.9 %copy-start.1 = (f32[3,8,8,512]{3,2,1,0:T(8,128)S(1)}, f32[3,8,8,512]{3,2,1,0:T(8,128)}, u32[]{:S(2)}) copy-start(f32[3,8,8,512]{3,2,1,0:T(8,128)} %own.3) | copy-start | bytes 1179652
  10.2 13.4 %copy-start.2 = (f32[3,8,8,512]{3,2,1,0:T(8,128)S(1)}, f32[3,8,8,512]{3,2,1,0:T(8,128)}, u32[]{:S(2)}) copy-start(f32[3,8,8,512]{3,2,1,0:T(8,128)} %own.2) | copy-start | bytes 1179652
  17.1 14.1 %all-to-all-start = ((f32[32,8,128]{2,1,0:T(8,128)}), f32[32,8,128]{2,1,0:T(8,128)S(1)}, u32[]{:S(2)}, u32[]{:S(2)}) async-start(f32[32,8,128]{2,1,0:T(8,128)} %shard_map.123), calls=%async_computation | async-start | bytes 262144 | tf_op jit(solution)/shard_map/all_to_all | solution.py:319
  23.6 16.7 %collective-permute-start.2 = (f32[3,512]{1,0:T(4,128)S(1)}, f32[3,512]{1,0:T(4,128)S(1)}, u32[]{:S(2)}, u32[]{:S(2)}) collective-permute-start(f32[3,512]{1,0:T(4,128)S(1)} %bitcast.26), channel_id=1, source_target_pairs={{9,0},{10,1},{11,2},{12,3},{13,4},{14,5},{15,6},{17,8},{18,9},{19,... | collective-permute-start | bytes 18440 | tf_op jit(solution)/shard_map/ppermute | solution.py:344
  27.0 2.1 %slice-start.1 = ((f32[3,8,8,512]{3,2,1,0:T(8,128)}), f32[3,8,1,512]{3,2,1,0:T(1,128)S(1)}, s32[]{:S(2)}) async-start(f32[3,8,8,512]{3,2,1,0:T(8,128)} %own.2), calls=%async_computation.3 | async-start | bytes 98304 | tf_op jit(solution)/shard_map/slice | solution.py:343
  27.0 13.3 %collective-permute-start = (f32[3,8,512]{2,1,0:T(8,128)S(1)}, f32[3,8,512]{2,1,0:T(8,128)S(1)}, u32[]{:S(2)}, u32[]{:S(2)}) collective-permute-start(f32[3,8,512]{2,1,0:T(8,128)S(1)} %slice_bitcast_fusion.1), channel_id=1, source_target_pairs={{8,0},{9,1},{10,2},{11,3},{12,4},{13,5},{14,6},{15,7},{16,8},{17,9... | collective-permute-start | bytes 147464 | tf_op jit(solution)/shard_map/ppermute | solution.py:342
  29.1 2.1 %copy-start.8 = (f32[3,512]{1,0:T(4,128)S(1)}, f32[3,512]{1,0:T(4,128)}, u32[]{:S(2)}) copy-start(f32[3,512]{1,0:T(4,128)} %points.1) | copy-start | bytes 18436
  29.1 2.1 %copy-start.9 = (s32[4,512]{1,0:T(4,128)S(1)}, s32[4,512]{1,0:T(4,128)}, u32[]{:S(2)}) copy-start(s32[4,512]{1,0:T(4,128)} %candidates.1) | copy-start | bytes 24580
  29.1 11.2 %copy-start.3 = (f32[6,8,8,512]{3,2,1,0:T(8,128)S(1)}, f32[6,8,8,512]{3,2,1,0:T(8,128)}, u32[]{:S(2)}) copy-start(f32[6,8,8,512]{3,2,1,0:T(8,128)} %stress.1) | copy-start | bytes 2359300
  29.1 11.2 %collective-permute-start.1 = (f32[3,8,512]{2,1,0:T(8,128)S(1)}, f32[3,8,512]{2,1,0:T(8,128)S(1)}, u32[]{:S(2)}, u32[]{:S(2)}) collective-permute-start(f32[3,8,512]{2,1,0:T(8,128)S(1)} %bitcast.24), channel_id=1, source_target_pairs={{1,0},{2,1},{3,2},{4,3},{5,4},{6,5},{7,6},{9,8},{10,9},{11,10},{12... | collective-permute-start | bytes 147464 | tf_op jit(solution)/shard_map/ppermute | solution.py:343
  33.7 6.6 %copy-start.4 = (f32[8,8,512]{2,1,0:T(8,128)S(1)}, f32[8,8,512]{2,1,0:T(8,128)}, u32[]{:S(2)}) copy-start(f32[8,8,512]{2,1,0:T(8,128)} %lame_lambda.1) | copy-start | bytes 393220
  33.7 6.7 %copy-start.5 = (f32[8,8,512]{2,1,0:T(8,128)S(1)}, f32[8,8,512]{2,1,0:T(8,128)}, u32[]{:S(2)}) copy-start(f32[8,8,512]{2,1,0:T(8,128)} %lame_mu.1) | copy-start | bytes 393220
  33.7 13.1 %all-to-all-start.1 = ((f32[32,8,128]{2,1,0:T(8,128)}), f32[32,8,128]{2,1,0:T(8,128)S(1)}, u32[]{:S(2)}, u32[]{:S(2)}) async-start(f32[32,8,128]{2,1,0:T(8,128)} %get-tuple-element.15), calls=%async_computation.1 | async-start | bytes 262144 | tf_op jit(solution)/shard_map/all_to_all | solution.py:319
  46.8 13.9 %copy-start = (f32[8,8,512]{2,1,0:T(8,128)S(1)}, f32[8,8,512]{2,1,0:T(8,128)}, u32[]{:S(2)}) copy-start(f32[8,8,512]{2,1,0:T(8,128)} %mass.1) | copy-start | bytes 393220
  49.4 11.3 %collective-permute-start.6 = (f32[3,8,512]{2,1,0:T(8,128)S(1)}, f32[3,8,512]{2,1,0:T(8,128)S(1)}, u32[]{:S(2)}, u32[]{:S(2)}) collective-permute-start(f32[3,8,512]{2,1,0:T(8,128)S(1)} %get-tuple-element.21), channel_id=1, source_target_pairs={{0,8},{1,9},{2,10},{3,11},{4,12},{5,13},{6,14},{7,15},{8,16},{9,17... | collective-permute-start | bytes 147464 | tf_op jit(solution)/shard_map/ppermute | solution.py:386
  52.3 8.4 %collective-permute-start.7 = (f32[3,8,512]{2,1,0:T(8,128)S(1)}, f32[3,8,512]{2,1,0:T(8,128)S(1)}, u32[]{:S(2)}, u32[]{:S(2)}) collective-permute-start(f32[3,8,512]{2,1,0:T(8,128)S(1)} %get-tuple-element.22), channel_id=1, source_target_pairs={{0,1},{1,2},{2,3},{3,4},{4,5},{5,6},{6,7},{8,9},{9,10},{10,11},{11... | collective-permute-start | bytes 147464 | tf_op jit(solution)/shard_map/ppermute | solution.py:387
  54.8 5.9 %collective-permute-start.8 = (f32[3,512]{1,0:T(4,128)S(1)}, f32[3,512]{1,0:T(4,128)S(1)}, u32[]{:S(2)}, u32[]{:S(2)}) collective-permute-start(f32[3,512]{1,0:T(4,128)S(1)} %get-tuple-element.23), channel_id=1, source_target_pairs={{0,9},{1,10},{2,11},{3,12},{4,13},{5,14},{6,15},{8,17},{9,18},{10,... | collective-permute-start | bytes 18440 | tf_op jit(solution)/shard_map/ppermute | solution.py:388

commit v2 on v1

--- a/solution.py
+++ b/solution.py
@@ -97,9 +97,8 @@
     return total
 
 
-def geometry_kernel(chunk, own, ghost_x, ghost_y, ghost_c, index, out, faces, payload):
+def geometry(chunk, own, ghost_x, ghost_y, ghost_c, index, groups, faces, payload):
     size_x, size_y, size_z = own.shape[1:]
-    groups = out.shape[0]
     count = index.shape[1]
 
     def plane(comp, i):
@@ -140,7 +139,7 @@
         part = values.astype(BF16).astype(F32)
         total += dot(spread(part, slot, groups).astype(BF16), hot_low, NT)
         total += dot(spread(values - part, slot, groups).astype(BF16), hot_low, NT)
-    out[...] = total.reshape(out.shape)
+    return total
 
 
 def stress_kernel(
@@ -201,10 +200,10 @@
         force_c[comp : comp + 1] = carry[comp][1]
 
 
-def contact_kernel(arrived, points, candidates, slave_force, reaction):
-    groups = arrived.shape[0]
+def contact(arrived, points, candidates, slave_force):
+    groups = arrived.shape[0] // 8
     lanes = points.shape[1]
-    high, low = two_terms(arrived[...].reshape(groups * 8, LANES))
+    high, low = two_terms(arrived)
     total = jnp.zeros((groups * 8, LANES), F32)
     pushed = [jnp.zeros((1, lanes), F32) for _ in range(3)]
     eight = lax.broadcasted_iota(jnp.int32, (8, lanes), 0)
@@ -230,17 +229,15 @@
         total += dot(spread(values - part, slot, groups).astype(BF16), hot, NT)
     for comp in range(3):
         slave_force[comp : comp + 1] = pushed[comp]
-    reaction[...] = total.reshape(reaction.shape)
-
-
-def nodes_kernel(
-    chunk, returned, index, in_force, in_x, in_y, in_c, force, force_x, force_y, force_c
-):
-    size_x, size_y, size_z = in_force.shape[1:]
-    groups = returned.shape[0]
+    return total
+
+
+def nodes_kernel(chunk, returned, index, force, force_x, force_y, force_c):
+    size_x, size_y, size_z = force.shape[1:]
+    groups = returned.shape[0] // 8
     count = index.shape[1]
     rows = size_x * size_y
-    high, low = two_terms(returned[...].reshape(groups * 8, LANES))
+    high, low = two_terms(returned)
     total = jnp.zeros((3 * rows, size_z), F32)
     for start in range(0, count, chunk):
         here = slice(start, start + chunk)
@@ -266,14 +263,14 @@
             value, value_end = both, end
             if before is not None:
                 value, value_end = both + before[0], end + before[1]
-            force[comp, i] = in_force[comp, i] + value
-            force_y[comp, i : i + 1] = in_y[comp, i : i + 1] + value_end
+            force[comp, i] = force[comp, i] + value
+            force_y[comp, i : i + 1] = force_y[comp, i : i + 1] + value_end
             before = (both, end)
-        force_x[comp] = in_x[comp] + before[0]
-        force_c[comp : comp + 1] = in_c[comp : comp + 1] + before[1]
-
-
-def final_kernel(force, from_x, from_y, from_c, mass, out):
+        force_x[comp] = force_x[comp] + before[0]
+        force_c[comp : comp + 1] = force_c[comp : comp + 1] + before[1]
+
+
+def final_kernel(force, from_x, from_y, from_c, mass):
     size_x = force.shape[1]
     first = lax.broadcasted_iota(jnp.int32, force.shape[2:], 0) == 0
     for i in range(size_x):
@@ -284,43 +281,152 @@
             if i == 0:
                 end = end + from_c[comp : comp + 1]
                 value = value + from_x[comp]
-            out[comp, i] = (value + jnp.where(first, end, 0.0)) * inverse
-
-
-def call(kernel, outs, *args, scratch=(), flops=0):
-    moved = sum(a.size * 4 for a in args) + sum(4 * functools.reduce(lambda x, y: x * y, s) for s, _ in outs)
-    return pl.pallas_call(
-        kernel,
-        out_shape=[jax.ShapeDtypeStruct(s, d) for s, d in outs],
-        in_specs=[VMEM] * len(args),
-        out_specs=[VMEM] * len(outs),
-        scratch_shapes=list(scratch),
-        compiler_params=pltpu.CompilerParams(vmem_limit_bytes=48 * 1024 * 1024),
-        cost_estimate=pl.CostEstimate(flops=flops, bytes_accessed=moved, transcendentals=0),
-    )(*args)
-
-
-def moves(count_x, count_y, by_x, by_y):
-    pairs = []
-    for x in range(count_x):
-        for y in range(count_y):
-            to_x, to_y = x + by_x, y + by_y
-            if 0 <= to_x < count_x and 0 <= to_y < count_y:
-                pairs.append((x * count_y + y, to_x * count_y + to_y))
-    return pairs
-
-
-def exchange(slots, devices):
-    groups, rows, lanes = slots.shape
-    per = devices // groups
-    if per > 1:
-        slots = slots.reshape(groups, rows, per, lanes // per).transpose(0, 2, 1, 3)
-        slots = slots.reshape(devices, rows, lanes // per)
-    slots = lax.all_to_all(slots, ("gx", "gy"), split_axis=0, concat_axis=0, tiled=True)
-    if per > 1:
-        slots = slots.reshape(groups, per, rows, lanes // per).transpose(0, 2, 1, 3)
-        slots = slots.reshape(groups, rows, lanes)
-    return slots
+            force[comp, i] = (value + jnp.where(first, end, 0.0)) * inverse
+
+
+def to_messages(total, messages):
+    devices, rows, capacity = messages.shape
+    per = LANES // capacity
+    if per == 1:
+        messages[...] = total.reshape(messages.shape)
+        return
+    for device in range(devices):
+        group, part = device // per, device % per
+        messages[device] = total[
+            group * rows : (group + 1) * rows, part * capacity : (part + 1) * capacity
+        ]
+
+
+def from_messages(messages):
+    devices, rows, capacity = messages.shape
+    per = LANES // capacity
+    if per == 1:
+        return messages[...].reshape(devices * rows, LANES)
+    return jnp.concatenate(
+        [
+            jnp.concatenate([messages[group * per + part] for part in range(per)], 1)
+            for group in range(devices // per)
+        ],
+        0,
+    )
+
+
+def fused_kernel(
+    count_x, count_y, chunk,
+    disp, vel, stress, lame_lambda, lame_mu, mass, elem, bucket, points, candidates,
+    new_stress, acceleration, slave_force,
+    index, faces, payload,
+    disp_x, disp_y, disp_c, vel_x, vel_y, vel_c,
+    disp_row, disp_edge, vel_row, vel_edge,
+    slots_out, slots_in, back_out, back_in,
+    force_x, force_y, force_c, from_x, from_y, from_c,
+    halo_send, halo_recv, force_send, force_recv, slot_send, slot_recv,
+):
+    devices = count_x * count_y
+    _, size_x, size_y, size_z = vel.shape
+    capacity = slots_out.shape[2]
+    at_x, at_y = lax.axis_index("gx"), lax.axis_index("gy")
+    me = at_x * count_y + at_y
+
+    def peer(step):
+        other = lax.rem(me + step, devices)
+        return other, (lax.div(other, count_y), lax.rem(other, count_y))
+
+    def remote(src, dst, send, recv, to):
+        return pltpu.make_async_remote_copy(
+            src_ref=src, dst_ref=dst, send_sem=send, recv_sem=recv,
+            device_id=to, device_id_type=pl.DeviceIdType.MESH,
+        )
+
+    barrier = pltpu.get_barrier_semaphore()
+
+    @pl.loop(1, devices)
+    def _(step):
+        pl.semaphore_signal(
+            barrier, inc=1, device_id=peer(step)[1], device_id_type=pl.DeviceIdType.MESH
+        )
+
+    for own, row, edge in ((disp, disp_row, disp_edge), (vel, vel_row, vel_edge)):
+        for comp in range(3):
+            for i in range(size_x):
+                row[comp, i : i + 1] = own[comp, i, 0:1]
+            edge[comp : comp + 1] = own[comp, 0, 0:1]
+    pl.semaphore_wait(barrier, devices - 1)
+
+    down_x, down_y = at_x > 0, at_y > 0
+    up_x, up_y = at_x < count_x - 1, at_y < count_y - 1
+    below = ((at_x - 1, at_y), (at_x, at_y - 1), (at_x - 1, at_y - 1))
+    above = ((at_x + 1, at_y), (at_x, at_y + 1), (at_x + 1, at_y + 1))
+    has_below = (down_x, down_y, jnp.logical_and(down_x, down_y))
+    has_above = (up_x, up_y, jnp.logical_and(up_x, up_y))
+
+    halo_in = (
+        (disp.at[:, 0], disp_x), (disp_row, disp_y), (disp_edge, disp_c),
+        (vel.at[:, 0], vel_x), (vel_row, vel_y), (vel_edge, vel_c),
+    )
+    halo_out = ((force_x, from_x), (force_y, from_y), (force_c, from_c))
+
+    def start(copies, sends, recvs, to, allowed):
+        for n, (src, dst) in enumerate(copies):
+            @pl.when(allowed[n % 3])
+            def _():
+                remote(src, dst, sends.at[n], recvs.at[n], to[n % 3]).start()
+
+    def finish(copies, sends, recvs, to, sent, got, which):
+        for n in which:
+            src, dst = copies[n]
+
+            @pl.when(got[n % 3])
+            def _():
+                remote(src, dst, sends.at[n], recvs.at[n], to[n % 3]).wait_recv()
+
+            @pl.when(sent[n % 3])
+            def _():
+                remote(src, dst, sends.at[n], recvs.at[n], to[n % 3]).wait_send()
+
+            @pl.when(jnp.logical_not(got[n % 3]))
+            def _():
+                dst[...] = jnp.zeros(dst.shape, F32)
+
+    def scatter(outgoing, incoming, n):
+        @pl.loop(1, devices)
+        def _(step):
+            other, to = peer(step)
+            remote(
+                outgoing.at[other], incoming.at[me], slot_send.at[n], slot_recv.at[n], to
+            ).start()
+
+        incoming[me] = outgoing[me]
+
+    def gather(outgoing, incoming, n):
+        most = pl.ds(0, devices - 1)
+        whole = remote(
+            outgoing.at[most], incoming.at[most], slot_send.at[n], slot_recv.at[n], peer(1)[1]
+        )
+        whole.wait_send()
+        whole.wait_recv()
+
+    start(halo_in, halo_send, halo_recv, below, has_below)
+    index_kernel(devices, capacity, size_z, elem, bucket, index)
+    finish(halo_in, halo_send, halo_recv, below, has_below, has_above, (0, 1, 2))
+    to_messages(
+        geometry(chunk, disp, disp_x, disp_y, disp_c, index, devices * capacity // LANES, faces, payload),
+        slots_out,
+    )
+    scatter(slots_out, slots_in, 0)
+    finish(halo_in, halo_send, halo_recv, below, has_below, has_above, (3, 4, 5))
+    stress_kernel(
+        vel, vel_x, vel_y, vel_c, stress, lame_lambda, lame_mu,
+        new_stress, acceleration, force_x, force_y, force_c,
+    )
+    gather(slots_out, slots_in, 0)
+    to_messages(contact(from_messages(slots_in), points, candidates, slave_force), back_out)
+    scatter(back_out, back_in, 1)
+    gather(back_out, back_in, 1)
+    nodes_kernel(chunk, from_messages(back_in), index, acceleration, force_x, force_y, force_c)
+    start(halo_out, force_send, force_recv, above, has_above)
+    finish(halo_out, force_send, force_recv, above, has_above, has_below, (0, 1, 2))
+    final_kernel(acceleration, from_x, from_y, from_c, mass)
 
 
 def per_device(
@@ -333,62 +439,34 @@
     _, size_x, size_y, size_z = velocity.shape
     seg_count = seg_elem.shape[0]
     capacity = 2 * seg_count // devices
-    slots = devices * capacity
-    groups = slots // LANES
-    axes = ("gx", "gy")
-
-    def ghosts(own):
-        return (
-            lax.ppermute(own[:, 0], axes, moves(count_x, count_y, -1, 0)),
-            lax.ppermute(own[:, :, 0], axes, moves(count_x, count_y, 0, -1)),
-            lax.ppermute(own[:, 0, 0], axes, moves(count_x, count_y, -1, -1)),
-        )
-
-    disp_ghosts = ghosts(displacement)
-    vel_ghosts = ghosts(velocity)
-    (index,) = call(
-        functools.partial(index_kernel, devices, capacity, size_z),
-        [((8, seg_count), jnp.int32)],
-        seg_elem.reshape(1, seg_count),
-        seg_bucket.reshape(1, seg_count),
-        flops=4_000_000_000,
-    )
     chunk = min(512, seg_count)
-    (outgoing,) = call(
-        functools.partial(geometry_kernel, chunk),
-        [((groups, 8, LANES), F32)],
-        displacement, *disp_ghosts, index,
-        scratch=[pltpu.VMEM((6, size_x, size_y, size_z), F32), pltpu.VMEM((8, chunk), F32)],
-        flops=4_000_000_000,
-    )
-    arrived = exchange(outgoing, devices)
-    plane = (3, size_y, size_z)
-    planes = [
-        (velocity.shape, F32), (plane, F32), ((3, size_x, size_z), F32), ((3, size_z), F32)
-    ]
-    new_stress, *forces = call(
-        stress_kernel,
-        [(stress.shape, F32)] + planes,
-        velocity, *vel_ghosts, stress, lame_lambda, lame_mu,
-        flops=8_000_000_000,
-    )
-    slave_force, reaction = call(
-        contact_kernel,
-        [(slave_points.shape, F32), ((groups, 8, LANES), F32)],
-        arrived, slave_points, candidates,
-        flops=2_000_000_000,
-    )
-    returned = exchange(reaction, devices)
-    force, force_x, force_y, force_c = call(
-        functools.partial(nodes_kernel, chunk), planes, returned, index, *forces,
-        flops=4_000_000_000,
-    )
-    from_x = lax.ppermute(force_x, axes, moves(count_x, count_y, 1, 0))
-    from_y = lax.ppermute(force_y, axes, moves(count_x, count_y, 0, 1))
-    from_c = lax.ppermute(force_c, axes, moves(count_x, count_y, 1, 1))
-    (acceleration,) = call(
-        final_kernel, [(velocity.shape, F32)], force, from_x, from_y, from_c, node_mass
-    )
+    args = (
+        displacement, velocity, stress, lame_lambda, lame_mu, node_mass,
+        seg_elem.reshape(1, seg_count), seg_bucket.reshape(1, seg_count),
+        slave_points, candidates,
+    )
+    outs = (stress.shape, velocity.shape, slave_points.shape)
+    side_x, side_y, side_c = (3, size_y, size_z), (3, size_x, size_z), (3, size_z)
+    message = (devices, 8, capacity)
+    shapes = (
+        [(6, size_x, size_y, size_z), (8, chunk)]
+        + [side_x, side_y, side_c] * 2
+        + [side_y, side_c] * 2
+        + [message] * 4
+        + [side_x, side_y, side_c] * 2
+    )
+    new_stress, acceleration, slave_force = pl.pallas_call(
+        functools.partial(fused_kernel, count_x, count_y, chunk),
+        out_shape=[jax.ShapeDtypeStruct(s, F32) for s in outs],
+        in_specs=[VMEM] * len(args),
+        out_specs=[VMEM] * len(outs),
+        scratch_shapes=[pltpu.VMEM((8, seg_count), jnp.int32)]
+        + [pltpu.VMEM(s, F32) for s in shapes]
+        + [pltpu.SemaphoreType.DMA((n,)) for n in (6, 6, 3, 3, 2, 2)],
+        compiler_params=pltpu.CompilerParams(
+            collective_id=0, has_side_effects=True, vmem_limit_bytes=48 * 1024 * 1024
+        ),
+    )(*args)
     return (new_stress, acceleration, slave_force)
 
 

time: 62.6 us -> 43.3 us (0.69)
  starting transfers between devices: 36.7 us -> 0 us
  Pallas kernels: 12.4 us -> 31.3 us
  waiting for transfers between devices: 9.73 us -> 0 us
  local copies, waits for them, and re-layouts: 1.71 us -> 10.8 us
    ppermute x9 -> x0, starting transfers between devices: 23.6 us -> none  [the longest x2 6.89 us: ghosts(): lax.ppermute(own[:, 0, 0], axes, moves(count_x, count_y, -1, -1))]
    pallas_call x6 -> x1, Pallas kernels: 12.4 us -> 31.3 us  [per_device(): pl.pallas_call(functools.partial(fused_kernel, count_x, count_y, chunk),...]
    all_to_all x2 -> x0, starting transfers between devices: 13.1 us -> none  [exchange(): lax.all_to_all(slots, ('gx', 'gy'), split_axis=0, concat_axis=0, tiled=True)]
    unnamed x24 -> x23, local copies, waits for them, and re-layouts: 0.07 us -> 10.8 us
    ppermute x9 -> x0, waiting for transfers between devices: 5.14 us -> none  [the longest x1 2.62 us: per_device(): from_c = lax.ppermute(force_c, axes, moves(count_x, count_y, 1, 1))]
    all_to_all x2 -> x0, waiting for transfers between devices: 4.59 us -> none  [exchange(): lax.all_to_all(slots, ('gx', 'gy'), split_axis=0, concat_axis=0, tiled=True)]
    slice x6 -> x0, local copies, waits for them, and re-layouts: 0.82 us -> none  [the longest x2 0.81 us: ghosts(): own[:, 0, 0]]
    squeeze x2 -> x0, local copies, waits for them, and re-layouts: 0.81 us -> none  [ghosts(): own[:, 0]]
  transfers between devices with their start and end apart: 11 -> 0, of which waited for: 4 -> 0; matrix products, arithmetic and copies ran while one was open for 1% -> 0% of each run, Pallas kernels for 8% -> 0%
where the time goes in v2:
time: 43.3 us; the launch traced here: 42.8 us
  Pallas kernels  31.3 us (72%)
  local copies, waits for them, and re-layouts  10.8 us (25%)
  between operations  0.66 us (2%)
    pallas_call x1, Pallas kernels, per_device(): pl.pallas_call(functools.partial(fused_kernel, count_x, count_y, chunk),...  31.3 us
    unnamed x23, local copies, waits for them, and re-layouts  10.8 us

profile of v2, /device:TPU:9, one launch (start us, length us, event | category | flops | bytes accessed | tf_op | source)
XLA Modules:
  0.0 42.8 jit_solution(10081896352218662292)
XLA Ops:
  0.6 0.0 copy-start
  0.6 1.1 %copy-done = f32[6,8,8,512]{3,2,1,0:T(8,128)S(1)} copy-done((f32[6,8,8,512]{3,2,1,0:T(8,128)S(1)}, f32[6,8,8,512]{3,2,1,0:T(8,128)}, u32[]{:S(2)}) %copy-start) | copy-done | bytes 786456
  1.8 0.0 copy-start.1
  1.8 1.0 %copy-done.1 = f32[3,8,8,512]{3,2,1,0:T(8,128)S(1)} copy-done((f32[3,8,8,512]{3,2,1,0:T(8,128)S(1)}, f32[3,8,8,512]{3,2,1,0:T(8,128)}, u32[]{:S(2)}) %copy-start.1) | copy-done | bytes 393240
  2.8 0.0 copy-start.2
  2.8 1.0 %copy-done.2 = f32[3,8,8,512]{3,2,1,0:T(8,128)S(1)} copy-done((f32[3,8,8,512]{3,2,1,0:T(8,128)S(1)}, f32[3,8,8,512]{3,2,1,0:T(8,128)}, u32[]{:S(2)}) %copy-start.2) | copy-done | bytes 393240
  3.8 0.0 copy-start.3
  3.8 0.9 %copy-done.3 = f32[8,8,512]{2,1,0:T(8,128)S(1)} copy-done((f32[8,8,512]{2,1,0:T(8,128)S(1)}, f32[8,8,512]{2,1,0:T(8,128)}, u32[]{:S(2)}) %copy-start.3) | copy-done | bytes 131096
  4.7 0.0 copy-start.4
  4.7 0.9 %copy-done.4 = f32[8,8,512]{2,1,0:T(8,128)S(1)} copy-done((f32[8,8,512]{2,1,0:T(8,128)S(1)}, f32[8,8,512]{2,1,0:T(8,128)}, u32[]{:S(2)}) %copy-start.4) | copy-done | bytes 131096
  5.6 0.0 copy-start.5
  5.6 0.9 %copy-done.5 = f32[8,8,512]{2,1,0:T(8,128)S(1)} copy-done((f32[8,8,512]{2,1,0:T(8,128)S(1)}, f32[8,8,512]{2,1,0:T(8,128)}, u32[]{:S(2)}) %copy-start.5) | copy-done | bytes 131096
  6.5 0.0 copy-start.6
  6.5 0.7 %copy-done.6 = s32[2048]{0:T(1024)S(1)} copy-done((s32[2048]{0:T(1024)S(1)}, s32[2048]{0:T(1024)}, u32[]{:S(2)}) %copy-start.6) | copy-done | bytes 8216
  7.2 0.0 copy-start.7
  7.2 0.7 %copy-done.7 = s32[2048,1]{0,1:T(1,128)S(1)} copy-done((s32[2048,1]{0,1:T(1,128)S(1)}, s32[2048,1]{0,1:T(1,128)}, u32[]{:S(2)}) %copy-start.7) | copy-done | bytes 8216
  7.9 0.0 copy-start.8
  7.9 0.7 %copy-done.8 = f32[3,512]{1,0:T(4,128)S(1)} copy-done((f32[3,512]{1,0:T(4,128)S(1)}, f32[3,512]{1,0:T(4,128)}, u32[]{:S(2)}) %copy-start.8) | copy-done | bytes 6168
  8.6 0.0 copy-start.9
  8.6 0.7 %copy-done.9 = s32[4,512]{1,0:T(4,128)S(1)} copy-done((s32[4,512]{1,0:T(4,128)S(1)}, s32[4,512]{1,0:T(4,128)}, u32[]{:S(2)}) %copy-start.9) | copy-done | bytes 8216
  9.3 31.3 %shard_map.121 = (f32[6,8,8,512]{3,2,1,0:T(8,128)S(1)}, f32[3,8,8,512]{3,2,1,0:T(8,128)S(1)}, f32[3,512]{1,0:T(4,128)S(1)}) custom-call(f32[3,8,8,512]{3,2,1,0:T(8,128)S(1)} %copy-done.1, f32[3,8,8,512]{3,2,1,0:T(8,128)S(1)} %copy-done.2, f32[6,8,8,512]{3,2,1,0:T(8,128)S(1)} %copy-done, f32[8,8,512]{2,1,0:T(8,128)S(1)} %copy-done.3, ...), custom_call_target="tpu_custom_call" | custom-call | tf_op jit(solution)/shard_map/pallas_call | solution.py:458
  40.6 0.9 %copy.16 = f32[6,8,8,512]{3,2,1,0:T(8,128)} copy(f32[6,8,8,512]{3,2,1,0:T(8,128)S(1)} %get-tuple-element.6) | data formatting | bytes 1572864
  41.5 0.7 %copy.17 = f32[3,8,8,512]{3,2,1,0:T(8,128)} copy(f32[3,8,8,512]{3,2,1,0:T(8,128)S(1)} %get-tuple-element.7) | data formatting | bytes 786432
  42.2 0.6 %copy.18 = f32[3,512]{1,0:T(4,128)} copy(f32[3,512]{1,0:T(4,128)S(1)} %get-tuple-element.8) | data formatting | bytes 12288
Async XLA Ops:
  0.6 1.1 %copy-start = (f32[6,8,8,512]{3,2,1,0:T(8,128)S(1)}, f32[6,8,8,512]{3,2,1,0:T(8,128)}, u32[]{:S(2)}) copy-start(f32[6,8,8,512]{3,2,1,0:T(8,128)} %stress.1) | copy-start | bytes 2359300
  1.8 1.0 %copy-start.1 = (f32[3,8,8,512]{3,2,1,0:T(8,128)S(1)}, f32[3,8,8,512]{3,2,1,0:T(8,128)}, u32[]{:S(2)}) copy-start(f32[3,8,8,512]{3,2,1,0:T(8,128)} %disp.1) | copy-start | bytes 1179652
  2.8 1.0 %copy-start.2 = (f32[3,8,8,512]{3,2,1,0:T(8,128)S(1)}, f32[3,8,8,512]{3,2,1,0:T(8,128)}, u32[]{:S(2)}) copy-start(f32[3,8,8,512]{3,2,1,0:T(8,128)} %vel.1) | copy-start | bytes 1179652
  3.8 0.9 %copy-start.3 = (f32[8,8,512]{2,1,0:T(8,128)S(1)}, f32[8,8,512]{2,1,0:T(8,128)}, u32[]{:S(2)}) copy-start(f32[8,8,512]{2,1,0:T(8,128)} %lame_lambda.1) | copy-start | bytes 393220
  4.7 0.9 %copy-start.4 = (f32[8,8,512]{2,1,0:T(8,128)S(1)}, f32[8,8,512]{2,1,0:T(8,128)}, u32[]{:S(2)}) copy-start(f32[8,8,512]{2,1,0:T(8,128)} %lame_mu.1) | copy-start | bytes 393220
  5.6 0.9 %copy-start.5 = (f32[8,8,512]{2,1,0:T(8,128)S(1)}, f32[8,8,512]{2,1,0:T(8,128)}, u32[]{:S(2)}) copy-start(f32[8,8,512]{2,1,0:T(8,128)} %mass.1) | copy-start | bytes 393220
  6.5 0.7 %copy-start.6 = (s32[2048]{0:T(1024)S(1)}, s32[2048]{0:T(1024)}, u32[]{:S(2)}) copy-start(s32[2048]{0:T(1024)} %param.16) | copy-start | bytes 24580
  7.2 0.7 %copy-start.7 = (s32[2048,1]{0,1:T(1,128)S(1)}, s32[2048,1]{0,1:T(1,128)}, u32[]{:S(2)}) copy-start(s32[2048,1]{0,1:T(1,128)} %param.17) | copy-start | bytes 24580
  7.9 0.7 %copy-start.8 = (f32[3,512]{1,0:T(4,128)S(1)}, f32[3,512]{1,0:T(4,128)}, u32[]{:S(2)}) copy-start(f32[3,512]{1,0:T(4,128)} %points.1) | copy-start | bytes 18436
  8.6 0.7 %copy-start.9 = (s32[4,512]{1,0:T(4,128)S(1)}, s32[4,512]{1,0:T(4,128)}, u32[]{:S(2)}) copy-start(s32[4,512]{1,0:T(4,128)} %candidates.1) | copy-start | bytes 24580

commit v3 on v2

--- a/solution.py
+++ b/solution.py
@@ -13,6 +13,7 @@
 F32 = jnp.float32
 BF16 = jnp.bfloat16
 VMEM = pl.BlockSpec(memory_space=pltpu.VMEM)
+HBM = pl.BlockSpec(memory_space=pltpu.HBM)
 NN = (((1,), (0,)), ((), ()))
 NT = (((1,), (1,)), ((), ()))
 
@@ -58,11 +59,17 @@
     return jnp.where(lax.broadcasted_iota(jnp.int32, tile.shape, 1) == 0, 0.0, rolled)
 
 
-def index_kernel(devices, capacity, size_z, elem, bucket, out):
+def index_kernel(devices, capacity, size_x, size_y, size_z, elem, bucket, out):
     count = elem.shape[1]
     row, depth = split_index(elem[...], size_z)
+    cell_i, cell_j = split_index(row, size_y)
+    ends = cell_j == size_y - 1
     out[0:1] = depth + 1
     out[1:2] = row
+    out[4:5] = jnp.where(ends, -1, row)
+    out[5:6] = row - (size_x - 1) * size_y
+    out[6:7] = jnp.where(ends & (cell_i < size_x - 1), cell_i, -1)
+    out[7:8] = jnp.zeros((1, count), jnp.int32)
     tri = (
         lax.broadcasted_iota(jnp.int32, (LANES, LANES), 0)
         <= lax.broadcasted_iota(jnp.int32, (LANES, LANES), 1)
@@ -78,7 +85,6 @@
         high, low = split_index(target, LANES)
         out[2:3, start : start + LANES] = high
         out[3:4, start : start + LANES] = low
-    out[4:8] = jnp.zeros((4, count), jnp.int32)
 
 
 def spread(values, high, groups):
@@ -97,48 +103,88 @@
     return total
 
 
-def geometry(chunk, own, ghost_x, ghost_y, ghost_c, index, groups, faces, payload):
+def face_values(low, high, low_next, high_next):
+    mean = [0.25 * ((low[c] + high[c]) + (low_next[c] + high_next[c])) for c in range(3)]
+    p = [high_next[c] - low[c] for c in range(3)]
+    q = [low_next[c] - high[c] for c in range(3)]
+    return mean + [
+        0.5 * ((1.0 + p[1]) * q[2] - p[2] * (1.0 + q[1])),
+        0.5 * (p[2] * (q[0] - 1.0) - (1.0 + p[0]) * q[2]),
+        0.5 * (p[0] + p[1] + q[1] - q[0] + p[0] * q[1] - p[1] * q[0]),
+    ]
+
+
+def chosen(table, hot_row, at):
+    rows = hot_row.shape[0]
+    return jnp.sum(jnp.where(hot_row, table[at : at + rows], 0.0), axis=0, keepdims=True)
+
+
+def bf16_hot(row, count):
+    return one_hot(row, count).astype(F32).astype(BF16)
+
+
+def inner_faces(chunk, own, index, faces, payload, hot_depth, hot_low):
     size_x, size_y, size_z = own.shape[1:]
     count = index.shape[1]
-
-    def plane(comp, i):
-        return own[comp, i] if i < size_x else ghost_x[comp]
-
-    def last_row(comp, i):
-        return ghost_y[comp, i : i + 1] if i < size_x else ghost_c[comp : comp + 1]
-
-    for i in range(size_x):
-        p, q = [], []
-        for comp in range(3):
-            low, high = plane(comp, i), plane(comp, i + 1)
-            low_next = next_row(low, last_row(comp, i))
-            high_next = next_row(high, last_row(comp, i + 1))
-            faces[comp, i] = 0.25 * ((low + high) + (low_next + high_next))
-            p.append(high_next - low)
-            q.append(low_next - high)
-        faces[3, i] = 0.5 * ((1.0 + p[1]) * q[2] - p[2] * (1.0 + q[1]))
-        faces[4, i] = 0.5 * (p[2] * (q[0] - 1.0) - (1.0 + p[0]) * q[2])
-        faces[5, i] = 0.5 * (p[0] + p[1] + q[1] - q[0] + p[0] * q[1] - p[1] * q[0])
-    rows = size_x * size_y
+    for i in range(size_x - 1):
+        low = [own[c, i] for c in range(3)]
+        high = [own[c, i + 1] for c in range(3)]
+        after = [pltpu.roll(t, size_y - 1, 0) for t in low]
+        high_after = [pltpu.roll(t, size_y - 1, 0) for t in high]
+        for number, value in enumerate(face_values(low, high, after, high_after)):
+            faces[number, i] = value
+    rows = (size_x - 1) * size_y
     high, low = two_terms(faces[...].reshape(6 * rows, size_z))
-    total = jnp.zeros((groups * 8, LANES), F32)
-    payload[6:7] = jnp.ones((1, chunk), F32)
-    payload[7:8] = jnp.zeros((1, chunk), F32)
     for start in range(0, count, chunk):
         here = slice(start, start + chunk)
-        hot = one_hot(index[0:1, here], size_z).astype(F32).astype(BF16)
+        hot = bf16_hot(index[0:1, here], size_z)
+        hot_depth[:, here] = hot
+        hot_low[:, here] = bf16_hot(index[3:4, here], LANES)
         near = dot(high, hot, NN) + dot(low, hot, NN)
-        hot_row = one_hot(index[1:2, here], rows)
+        hot_row = one_hot(index[4:5, here], rows)
         for comp in range(6):
-            payload[comp : comp + 1] = jnp.sum(
-                jnp.where(hot_row, near[comp * rows : (comp + 1) * rows], 0.0), axis=0, keepdims=True
+            payload[comp : comp + 1, here] = chosen(near, hot_row, comp * rows)
+    payload[6:7] = jnp.ones((1, count), F32)
+    payload[7:8] = jnp.zeros((1, count), F32)
+
+
+def all_faces(
+    chunk, own, own_last, ghost_x, ghost_y, ghost_c, index, groups, edges, payload, hot_depth, hot_low
+):
+    size_x, size_y, size_z = own.shape[1:]
+    count = index.shape[1]
+    low = [own[c, size_x - 1] for c in range(3)]
+    high = [ghost_x[c] for c in range(3)]
+    after = [next_row(low[c], ghost_y[c, size_x - 1 : size_x]) for c in range(3)]
+    high_after = [next_row(high[c], ghost_c[c : c + 1]) for c in range(3)]
+    at = 0
+    for value in face_values(low, high, after, high_after):
+        edges[at : at + size_y] = value
+        at += size_y
+    low = [own_last[c] for c in range(3)]
+    after = [ghost_y[c] for c in range(3)]
+    high = [pltpu.roll(t, size_x - 1, 0) for t in low]
+    high_after = [pltpu.roll(t, size_x - 1, 0) for t in after]
+    for value in face_values(low, high, after, high_after):
+        edges[at : at + size_x] = value
+        at += size_x
+    high, low = two_terms(edges[...])
+    total = jnp.zeros((groups * 8, LANES), F32)
+    for start in range(0, count, chunk):
+        here = slice(start, start + chunk)
+        hot = hot_depth[:, here]
+        near = dot(high, hot, NN) + dot(low, hot, NN)
+        hot_x = one_hot(index[5:6, here], size_y)
+        hot_y = one_hot(index[6:7, here], size_x)
+        for comp in range(6):
+            payload[comp : comp + 1, here] += chosen(near, hot_x, comp * size_y) + chosen(
+                near, hot_y, 6 * size_y + comp * size_x
             )
         slot = index[2:3, here]
-        hot_low = one_hot(index[3:4, here], LANES).astype(F32).astype(BF16)
-        values = payload[...]
+        values = payload[:, here]
         part = values.astype(BF16).astype(F32)
-        total += dot(spread(part, slot, groups).astype(BF16), hot_low, NT)
-        total += dot(spread(values - part, slot, groups).astype(BF16), hot_low, NT)
+        total += dot(spread(part, slot, groups).astype(BF16), hot_low[:, here], NT)
+        total += dot(spread(values - part, slot, groups).astype(BF16), hot_low[:, here], NT)
     return total
 
 
@@ -200,7 +246,7 @@
         force_c[comp : comp + 1] = carry[comp][1]
 
 
-def contact(arrived, points, candidates, slave_force):
+def contact(arrived, points, candidates, hot_slot, slave_force):
     groups = arrived.shape[0] // 8
     lanes = points.shape[1]
     high, low = two_terms(arrived)
@@ -208,8 +254,8 @@
     pushed = [jnp.zeros((1, lanes), F32) for _ in range(3)]
     eight = lax.broadcasted_iota(jnp.int32, (8, lanes), 0)
     for k in range(candidates.shape[0]):
-        slot, place = split_index(candidates[k : k + 1], LANES)
-        hot = one_hot(place, LANES).astype(F32).astype(BF16)
+        slot = split_index(candidates[k : k + 1], LANES)[0]
+        hot = hot_slot[k]
         near = picked(dot(high, hot, NN) + dot(low, hot, NN), slot, groups)
         rows = [near[r : r + 1] for r in range(7)]
         filled = rows[6]
@@ -232,7 +278,9 @@
     return total
 
 
-def nodes_kernel(chunk, returned, index, force, force_x, force_y, force_c):
+def nodes_kernel(
+    chunk, returned, index, hot_depth, hot_low, force, force_x, force_y, force_c
+):
     size_x, size_y, size_z = force.shape[1:]
     groups = returned.shape[0] // 8
     count = index.shape[1]
@@ -241,13 +289,13 @@
     total = jnp.zeros((3 * rows, size_z), F32)
     for start in range(0, count, chunk):
         here = slice(start, start + chunk)
-        hot_low = one_hot(index[3:4, here], LANES).astype(F32).astype(BF16)
-        near = picked(dot(high, hot_low, NN) + dot(low, hot_low, NN), index[2:3, here], groups)
+        place = hot_low[:, here]
+        near = picked(dot(high, place, NN) + dot(low, place, NN), index[2:3, here], groups)
         quarter = 0.25 * near
         part = quarter.astype(BF16).astype(F32)
         rest = quarter - part
         hot_row = one_hot(index[1:2, here], rows)
-        hot = one_hot(index[0:1, here], size_z).astype(F32).astype(BF16)
+        hot = hot_depth[:, here]
         for values in (part, rest):
             left = jnp.concatenate(
                 [jnp.where(hot_row, values[c : c + 1], 0.0) for c in range(3)], 0
@@ -270,7 +318,25 @@
         force_c[comp : comp + 1] = force_c[comp : comp + 1] + before[1]
 
 
-def final_kernel(force, from_x, from_y, from_c, mass):
+def final_kernel(
+    stress, pushed, force_in, from_x_in, from_y_in, from_c_in, mass_in,
+    new_stress, acceleration, slave_force,
+    force, from_x, from_y, from_c, mass, result, sems,
+):
+    copies = [
+        pltpu.make_async_copy(src, dst, sems.at[n])
+        for n, (src, dst) in enumerate(
+            (
+                (mass_in, mass), (force_in, force), (from_x_in, from_x), (from_y_in, from_y),
+                (from_c_in, from_c), (stress, new_stress), (pushed, slave_force),
+                (result, acceleration),
+            )
+        )
+    ]
+    for copy in copies[:7]:
+        copy.start()
+    for copy in copies[:5]:
+        copy.wait()
     size_x = force.shape[1]
     first = lax.broadcasted_iota(jnp.int32, force.shape[2:], 0) == 0
     for i in range(size_x):
@@ -281,7 +347,10 @@
             if i == 0:
                 end = end + from_c[comp : comp + 1]
                 value = value + from_x[comp]
-            force[comp, i] = (value + jnp.where(first, end, 0.0)) * inverse
+            result[comp, i] = (value + jnp.where(first, end, 0.0)) * inverse
+    copies[7].start()
+    for copy in copies[5:]:
+        copy.wait()
 
 
 def to_messages(total, messages):
@@ -313,18 +382,21 @@
 
 def fused_kernel(
     count_x, count_y, chunk,
-    disp, vel, stress, lame_lambda, lame_mu, mass, elem, bucket, points, candidates,
-    new_stress, acceleration, slave_force,
-    index, faces, payload,
+    disp_in, elem_in, bucket_in, vel_in, stress_in, lambda_in, mu_in, points_in, candidates_in,
+    stress_out, force, slave_force, from_x, from_y, from_c,
+    new_stress, disp, elem, bucket, vel, stress, lame_lambda, lame_mu, points, candidates,
+    index, hot_depth, hot_low, hot_slot, faces, edges, payload, disp_last,
     disp_x, disp_y, disp_c, vel_x, vel_y, vel_c,
     disp_row, disp_edge, vel_row, vel_edge,
     slots_out, slots_in, back_out, back_in,
-    force_x, force_y, force_c, from_x, from_y, from_c,
-    halo_send, halo_recv, force_send, force_recv, slot_send, slot_recv,
+    force_x, force_y, force_c,
+    load_sems, store_sem, halo_send, halo_recv, force_send, force_recv, slot_send, slot_recv,
 ):
     devices = count_x * count_y
     _, size_x, size_y, size_z = vel.shape
     capacity = slots_out.shape[2]
+    groups = devices * capacity // LANES
+    kept = (7, 3)
     at_x, at_y = lax.axis_index("gx"), lax.axis_index("gy")
     me = at_x * count_y + at_y
 
@@ -338,6 +410,18 @@
             device_id=to, device_id_type=pl.DeviceIdType.MESH,
         )
 
+    loads = [
+        pltpu.make_async_copy(src, dst, load_sems.at[n])
+        for n, (src, dst) in enumerate(
+            (
+                (disp_in, disp), (elem_in, elem), (bucket_in, bucket), (vel_in, vel),
+                (stress_in, stress), (lambda_in, lame_lambda), (mu_in, lame_mu),
+                (points_in, points), (candidates_in, candidates),
+            )
+        )
+    ]
+    for load in loads:
+        load.start()
     barrier = pltpu.get_barrier_semaphore()
 
     @pl.loop(1, devices)
@@ -346,11 +430,17 @@
             barrier, inc=1, device_id=peer(step)[1], device_id_type=pl.DeviceIdType.MESH
         )
 
-    for own, row, edge in ((disp, disp_row, disp_edge), (vel, vel_row, vel_edge)):
+    def pack(own, row, edge):
         for comp in range(3):
             for i in range(size_x):
                 row[comp, i : i + 1] = own[comp, i, 0:1]
             edge[comp : comp + 1] = own[comp, 0, 0:1]
+
+    loads[0].wait()
+    pack(disp, disp_row, disp_edge)
+    for comp in range(3):
+        for i in range(size_x):
+            disp_last[comp, i : i + 1] = disp[comp, i, size_y - 1 : size_y]
     pl.semaphore_wait(barrier, devices - 1)
 
     down_x, down_y = at_x > 0, at_y > 0
@@ -366,8 +456,10 @@
     )
     halo_out = ((force_x, from_x), (force_y, from_y), (force_c, from_c))
 
-    def start(copies, sends, recvs, to, allowed):
-        for n, (src, dst) in enumerate(copies):
+    def start(copies, sends, recvs, to, allowed, which):
+        for n in which:
+            src, dst = copies[n]
+
             @pl.when(allowed[n % 3])
             def _():
                 remote(src, dst, sends.at[n], recvs.at[n], to[n % 3]).start()
@@ -389,44 +481,65 @@
                 dst[...] = jnp.zeros(dst.shape, F32)
 
     def scatter(outgoing, incoming, n):
+        used = pl.ds(0, kept[n])
+
         @pl.loop(1, devices)
         def _(step):
             other, to = peer(step)
             remote(
-                outgoing.at[other], incoming.at[me], slot_send.at[n], slot_recv.at[n], to
+                outgoing.at[other, used], incoming.at[me, used], slot_send.at[n], slot_recv.at[n], to
             ).start()
 
         incoming[me] = outgoing[me]
 
     def gather(outgoing, incoming, n):
-        most = pl.ds(0, devices - 1)
+        most = (pl.ds(0, devices - 1), pl.ds(0, kept[n]))
         whole = remote(
             outgoing.at[most], incoming.at[most], slot_send.at[n], slot_recv.at[n], peer(1)[1]
         )
         whole.wait_send()
         whole.wait_recv()
 
-    start(halo_in, halo_send, halo_recv, below, has_below)
-    index_kernel(devices, capacity, size_z, elem, bucket, index)
-    finish(halo_in, halo_send, halo_recv, below, has_below, has_above, (0, 1, 2))
+    halo = (halo_in, halo_send, halo_recv, below)
+    start(*halo, has_below, (0, 1, 2))
+    loads[1].wait()
+    loads[2].wait()
+    index_kernel(devices, capacity, size_x, size_y, size_z, elem, bucket, index)
+    inner_faces(chunk, disp, index, faces, payload, hot_depth, hot_low)
+    finish(*halo, has_below, has_above, (0, 1, 2))
     to_messages(
-        geometry(chunk, disp, disp_x, disp_y, disp_c, index, devices * capacity // LANES, faces, payload),
+        all_faces(
+            chunk, disp, disp_last, disp_x, disp_y, disp_c, index, groups, edges, payload,
+            hot_depth, hot_low,
+        ),
         slots_out,
     )
     scatter(slots_out, slots_in, 0)
-    finish(halo_in, halo_send, halo_recv, below, has_below, has_above, (3, 4, 5))
+    loads[3].wait()
+    pack(vel, vel_row, vel_edge)
+    start(*halo, has_below, (3, 4, 5))
+    for load in loads[4:]:
+        load.wait()
+    for k in range(candidates.shape[0]):
+        hot_slot[k] = bf16_hot(split_index(candidates[k : k + 1], LANES)[1], LANES)
+    finish(*halo, has_below, has_above, (3, 4, 5))
     stress_kernel(
         vel, vel_x, vel_y, vel_c, stress, lame_lambda, lame_mu,
-        new_stress, acceleration, force_x, force_y, force_c,
-    )
+        new_stress, force, force_x, force_y, force_c,
+    )
+    store = pltpu.make_async_copy(new_stress, stress_out, store_sem)
+    store.start()
     gather(slots_out, slots_in, 0)
-    to_messages(contact(from_messages(slots_in), points, candidates, slave_force), back_out)
+    to_messages(contact(from_messages(slots_in), points, candidates, hot_slot, slave_force), back_out)
     scatter(back_out, back_in, 1)
     gather(back_out, back_in, 1)
-    nodes_kernel(chunk, from_messages(back_in), index, acceleration, force_x, force_y, force_c)
-    start(halo_out, force_send, force_recv, above, has_above)
-    finish(halo_out, force_send, force_recv, above, has_above, has_below, (0, 1, 2))
-    final_kernel(acceleration, from_x, from_y, from_c, mass)
+    nodes_kernel(
+        chunk, from_messages(back_in), index, hot_depth, hot_low, force, force_x, force_y, force_c
+    )
+    back = (halo_out, force_send, force_recv, above)
+    start(*back, has_above, (0, 1, 2))
+    finish(*back, has_above, has_below, (0, 1, 2))
+    store.wait()
 
 
 def per_device(
@@ -441,32 +554,52 @@
     capacity = 2 * seg_count // devices
     chunk = min(512, seg_count)
     args = (
-        displacement, velocity, stress, lame_lambda, lame_mu, node_mass,
-        seg_elem.reshape(1, seg_count), seg_bucket.reshape(1, seg_count),
-        slave_points, candidates,
-    )
-    outs = (stress.shape, velocity.shape, slave_points.shape)
+        displacement, seg_elem.reshape(1, seg_count), seg_bucket.reshape(1, seg_count),
+        velocity, stress, lame_lambda, lame_mu, slave_points, candidates,
+    )
     side_x, side_y, side_c = (3, size_y, size_z), (3, size_x, size_z), (3, size_z)
+    outs = (stress.shape, velocity.shape, slave_points.shape, side_x, side_y, side_c)
     message = (devices, 8, capacity)
+    scratch = [pltpu.VMEM(stress.shape, F32)] + [pltpu.VMEM(a.shape, a.dtype) for a in args]
+    scratch += [
+        pltpu.VMEM((8, seg_count), jnp.int32),
+        pltpu.VMEM((size_z, seg_count), BF16),
+        pltpu.VMEM((LANES, seg_count), BF16),
+        pltpu.VMEM((candidates.shape[0], LANES, candidates.shape[1]), BF16),
+    ]
     shapes = (
-        [(6, size_x, size_y, size_z), (8, chunk)]
+        [(6, size_x - 1, size_y, size_z), (6 * (size_x + size_y), size_z), (8, seg_count), side_y]
         + [side_x, side_y, side_c] * 2
         + [side_y, side_c] * 2
         + [message] * 4
-        + [side_x, side_y, side_c] * 2
-    )
-    new_stress, acceleration, slave_force = pl.pallas_call(
+        + [side_x, side_y, side_c]
+    )
+    scratch += [pltpu.VMEM(s, F32) for s in shapes]
+    scratch += [pltpu.SemaphoreType.DMA((len(args),)), pltpu.SemaphoreType.DMA]
+    scratch += [pltpu.SemaphoreType.DMA((n,)) for n in (6, 6, 3, 3, 2, 2)]
+    parts = pl.pallas_call(
         functools.partial(fused_kernel, count_x, count_y, chunk),
         out_shape=[jax.ShapeDtypeStruct(s, F32) for s in outs],
-        in_specs=[VMEM] * len(args),
-        out_specs=[VMEM] * len(outs),
-        scratch_shapes=[pltpu.VMEM((8, seg_count), jnp.int32)]
-        + [pltpu.VMEM(s, F32) for s in shapes]
-        + [pltpu.SemaphoreType.DMA((n,)) for n in (6, 6, 3, 3, 2, 2)],
+        in_specs=[HBM] * len(args),
+        out_specs=[HBM] + [VMEM] * (len(outs) - 1),
+        scratch_shapes=scratch,
         compiler_params=pltpu.CompilerParams(
-            collective_id=0, has_side_effects=True, vmem_limit_bytes=48 * 1024 * 1024
+            collective_id=0, has_side_effects=True, vmem_limit_bytes=60 * 1024 * 1024
         ),
     )(*args)
+    stress_part, force, pushed, *from_others = parts
+    new_stress, acceleration, slave_force = pl.pallas_call(
+        final_kernel,
+        out_shape=[jax.ShapeDtypeStruct(s, F32) for s in outs[:3]],
+        in_specs=[HBM] * 7,
+        out_specs=[HBM] * 3,
+        scratch_shapes=[
+            pltpu.VMEM(s, F32)
+            for s in (velocity.shape, side_x, side_y, side_c, node_mass.shape, velocity.shape)
+        ]
+        + [pltpu.SemaphoreType.DMA((8,))],
+        compiler_params=pltpu.CompilerParams(vmem_limit_bytes=60 * 1024 * 1024),
+    )(stress_part, pushed, force, *from_others, node_mass)
     return (new_stress, acceleration, slave_force)
 
 

time: 43.3 us -> 54.9 us (1.27)
  Pallas kernels: 31.3 us -> 54.1 us
  local copies, waits for them, and re-layouts: 10.8 us -> 0 us
    pallas_call x0 -> x1, Pallas kernels: none -> 25.3 us  [per_device(): pl.pallas_call(final_kernel, out_shape=[jax.ShapeDtypeStruct(s, F32) for...]
    unnamed x23 -> x0, local copies, waits for them, and re-layouts: 10.8 us -> none
    pallas_call x1, Pallas kernels: 31.3 us -> 28.8 us  [per_device(): pl.pallas_call(functools.partial(fused_kernel, count_x, count_y, chunk),...]
where the time goes in v3:
time: 54.9 us; the launch traced here: 54.7 us
  Pallas kernels  54.1 us (99%)
  between operations  0.64 us (1%)
    pallas_call x1, Pallas kernels, per_device(): pl.pallas_call(functools.partial(fused_kernel, count_x, count_y, chunk),...  28.8 us
    pallas_call x1, Pallas kernels, per_device(): pl.pallas_call(final_kernel, out_shape=[jax.ShapeDtypeStruct(s, F32) for...  25.3 us

profile of v3, /device:TPU:9, one launch (start us, length us, event | category | flops | bytes accessed | tf_op | source)
XLA Modules:
  0.0 54.7 jit_solution(2474834451256102955)
XLA Ops:
  0.6 28.8 %shard_map.121 = (f32[6,8,8,512]{3,2,1,0:T(8,128)}, f32[3,8,8,512]{3,2,1,0:T(8,128)}, f32[3,512]{1,0:T(4,128)}, f32[3,8,512]{2,1,0:T(8,128)}, f32[3,8,512]{2,1,0:T(8,128)}, /*index=5*/f32[3,512]{1,0:T(4,128)}) custom-call(f32[3,8,8,512]{3,2,1,0:T(8,128)} %disp_in.1, s32[1,2048]{1,0:T(1,128)} %bitcast.2, s32[1,2048]{1,0:T(1,128)} %bitcast.3, ...), custom_call_target="tpu_custom_call" | custom-call | tf_op jit(solution)/shard_map/pallas_call | solution.py:580
  29.5 25.3 %shard_map.122 = (f32[6,8,8,512]{3,2,1,0:T(8,128)}, f32[3,8,8,512]{3,2,1,0:T(8,128)}, f32[3,512]{1,0:T(4,128)}) custom-call(f32[6,8,8,512]{3,2,1,0:T(8,128)} %get-tuple-element.9.stress, f32[3,512]{1,0:T(4,128)} %get-tuple-element.10.pushed, f32[3,8,8,512]{3,2,1,0:T(8,128)} %get-tuple-element.11.force_in, f32[3,8,512]{2,1,0:T(8,128)} %get-tuple-element.12.from_x_in, ...), custom_call_target="tpu_custom_call" | custom-call | tf_op jit(solution)/shard_map/pallas_call | solution.py:591

commit v4 on v3

--- a/solution.py
+++ b/solution.py
@@ -31,6 +31,17 @@
 
 def dot(left, right, dims):
     return lax.dot_general(left, right, dims, preferred_element_type=F32)
+
+
+def stacked(terms, right, dims):
+    rows = terms.shape[0] // 2
+    both = dot(terms, right, dims)
+    return both[:rows] + both[rows:]
+
+
+def halves(total):
+    rows = total.shape[0] // 2
+    return total[:rows] + total[rows:]
 
 
 def one_hot(row, count):
@@ -94,6 +105,13 @@
     return kept.reshape(groups * rows, lanes)
 
 
+def spread_terms(values, high, groups):
+    part = values.astype(BF16).astype(F32)
+    return jnp.concatenate(
+        [spread(term, high, groups).astype(BF16) for term in (part, values - part)], 0
+    )
+
+
 def picked(table, high, groups):
     rows = table.shape[0] // groups
     lanes = table.shape[1]
@@ -168,12 +186,11 @@
     for value in face_values(low, high, after, high_after):
         edges[at : at + size_x] = value
         at += size_x
-    high, low = two_terms(edges[...])
-    total = jnp.zeros((groups * 8, LANES), F32)
+    terms = jnp.concatenate(two_terms(edges[...]), 0)
+    total = jnp.zeros((groups * 16, LANES), F32)
     for start in range(0, count, chunk):
         here = slice(start, start + chunk)
-        hot = hot_depth[:, here]
-        near = dot(high, hot, NN) + dot(low, hot, NN)
+        near = stacked(terms, hot_depth[:, here], NN)
         hot_x = one_hot(index[5:6, here], size_y)
         hot_y = one_hot(index[6:7, here], size_x)
         for comp in range(6):
@@ -182,10 +199,8 @@
             )
         slot = index[2:3, here]
         values = payload[:, here]
-        part = values.astype(BF16).astype(F32)
-        total += dot(spread(part, slot, groups).astype(BF16), hot_low[:, here], NT)
-        total += dot(spread(values - part, slot, groups).astype(BF16), hot_low[:, here], NT)
-    return total
+        total += dot(spread_terms(values, slot, groups), hot_low[:, here], NT)
+    return halves(total)
 
 
 def stress_kernel(
@@ -249,14 +264,14 @@
 def contact(arrived, points, candidates, hot_slot, slave_force):
     groups = arrived.shape[0] // 8
     lanes = points.shape[1]
-    high, low = two_terms(arrived)
-    total = jnp.zeros((groups * 8, LANES), F32)
+    terms = jnp.concatenate(two_terms(arrived), 0)
+    total = jnp.zeros((groups * 16, LANES), F32)
     pushed = [jnp.zeros((1, lanes), F32) for _ in range(3)]
     eight = lax.broadcasted_iota(jnp.int32, (8, lanes), 0)
     for k in range(candidates.shape[0]):
         slot = split_index(candidates[k : k + 1], LANES)[0]
         hot = hot_slot[k]
-        near = picked(dot(high, hot, NN) + dot(low, hot, NN), slot, groups)
+        near = picked(stacked(terms, hot, NN), slot, groups)
         rows = [near[r : r + 1] for r in range(7)]
         filled = rows[6]
         offset = (0.5, 0.5, 1.0)
@@ -270,12 +285,10 @@
             push = scale * area[comp]
             pushed[comp] = pushed[comp] + push
             values = jnp.where(eight == comp, -push, values)
-        part = values.astype(BF16).astype(F32)
-        total += dot(spread(part, slot, groups).astype(BF16), hot, NT)
-        total += dot(spread(values - part, slot, groups).astype(BF16), hot, NT)
+        total += dot(spread_terms(values, slot, groups), hot, NT)
     for comp in range(3):
         slave_force[comp : comp + 1] = pushed[comp]
-    return total
+    return halves(total)
 
 
 def nodes_kernel(
@@ -285,22 +298,25 @@
     groups = returned.shape[0] // 8
     count = index.shape[1]
     rows = size_x * size_y
-    high, low = two_terms(returned)
-    total = jnp.zeros((3 * rows, size_z), F32)
+    terms = jnp.concatenate(two_terms(returned), 0)
+    total = jnp.zeros((6 * rows, size_z), F32)
     for start in range(0, count, chunk):
         here = slice(start, start + chunk)
-        place = hot_low[:, here]
-        near = picked(dot(high, place, NN) + dot(low, place, NN), index[2:3, here], groups)
+        near = picked(stacked(terms, hot_low[:, here], NN), index[2:3, here], groups)
         quarter = 0.25 * near
         part = quarter.astype(BF16).astype(F32)
         rest = quarter - part
         hot_row = one_hot(index[1:2, here], rows)
-        hot = hot_depth[:, here]
-        for values in (part, rest):
-            left = jnp.concatenate(
-                [jnp.where(hot_row, values[c : c + 1], 0.0) for c in range(3)], 0
-            ).astype(BF16)
-            total += dot(left, hot, NT)
+        left = jnp.concatenate(
+            [
+                jnp.where(hot_row, values[c : c + 1], 0.0)
+                for values in (part, rest)
+                for c in range(3)
+            ],
+            0,
+        ).astype(BF16)
+        total += dot(left, hot_depth[:, here], NT)
+    total = halves(total)
     for comp in range(3):
         before = None
         for i in range(size_x):
@@ -321,21 +337,24 @@
 def final_kernel(
     stress, pushed, force_in, from_x_in, from_y_in, from_c_in, mass_in,
     new_stress, acceleration, slave_force,
-    force, from_x, from_y, from_c, mass, result, sems,
+    stress_here, pushed_here, force, from_x, from_y, from_c, mass, result, sems,
 ):
     copies = [
         pltpu.make_async_copy(src, dst, sems.at[n])
         for n, (src, dst) in enumerate(
             (
-                (mass_in, mass), (force_in, force), (from_x_in, from_x), (from_y_in, from_y),
-                (from_c_in, from_c), (stress, new_stress), (pushed, slave_force),
-                (result, acceleration),
+                (stress, stress_here), (pushed, pushed_here), (mass_in, mass), (force_in, force),
+                (from_x_in, from_x), (from_y_in, from_y), (from_c_in, from_c),
+                (stress_here, new_stress), (pushed_here, slave_force), (result, acceleration),
             )
         )
     ]
     for copy in copies[:7]:
         copy.start()
-    for copy in copies[:5]:
+    for n in (0, 1):
+        copies[n].wait()
+        copies[7 + n].start()
+    for copy in copies[2:7]:
         copy.wait()
     size_x = force.shape[1]
     first = lax.broadcasted_iota(jnp.int32, force.shape[2:], 0) == 0
@@ -348,8 +367,8 @@
                 end = end + from_c[comp : comp + 1]
                 value = value + from_x[comp]
             result[comp, i] = (value + jnp.where(first, end, 0.0)) * inverse
-    copies[7].start()
-    for copy in copies[5:]:
+    copies[9].start()
+    for copy in copies[7:]:
         copy.wait()
 
 
@@ -595,9 +614,9 @@
         out_specs=[HBM] * 3,
         scratch_shapes=[
             pltpu.VMEM(s, F32)
-            for s in (velocity.shape, side_x, side_y, side_c, node_mass.shape, velocity.shape)
+            for s in outs[:1] + outs[2:3] + (velocity.shape, side_x, side_y, side_c, node_mass.shape, velocity.shape)
         ]
-        + [pltpu.SemaphoreType.DMA((8,))],
+        + [pltpu.SemaphoreType.DMA((10,))],
         compiler_params=pltpu.CompilerParams(vmem_limit_bytes=60 * 1024 * 1024),
     )(stress_part, pushed, force, *from_others, node_mass)
     return (new_stress, acceleration, slave_force)

time: 54.9 us -> 31.7 us (0.58)
  Pallas kernels: 54.1 us -> 30.9 us
    pallas_call x1, Pallas kernels: 25.3 us -> 2.23 us  [per_device(): pl.pallas_call(final_kernel, out_shape=[jax.ShapeDtypeStruct(s, F32) for...]
where the time goes in v4:
time: 31.7 us; the launch traced here: 31.5 us
  Pallas kernels  30.9 us (97%)
  between operations  0.64 us (2%)
    pallas_call x1, Pallas kernels, per_device(): pl.pallas_call(functools.partial(fused_kernel, count_x, count_y, chunk),...  28.7 us
    pallas_call x1, Pallas kernels, per_device(): pl.pallas_call(final_kernel, out_shape=[jax.ShapeDtypeStruct(s, F32) for...  2.23 us

profile of v4, /device:TPU:9, one launch (start us, length us, event | category | flops | bytes accessed | tf_op | source)
XLA Modules:
  0.0 31.5 jit_solution(3193469148053912033)
XLA Ops:
  0.6 28.7 %shard_map.121 = (f32[6,8,8,512]{3,2,1,0:T(8,128)}, f32[3,8,8,512]{3,2,1,0:T(8,128)}, f32[3,512]{1,0:T(4,128)}, f32[3,8,512]{2,1,0:T(8,128)}, f32[3,8,512]{2,1,0:T(8,128)}, /*index=5*/f32[3,512]{1,0:T(4,128)}) custom-call(f32[3,8,8,512]{3,2,1,0:T(8,128)} %disp_in.1, s32[1,2048]{1,0:T(1,128)} %bitcast.2, s32[1,2048]{1,0:T(1,128)} %bitcast.3, ...), custom_call_target="tpu_custom_call" | custom-call | tf_op jit(solution)/shard_map/pallas_call | solution.py:599
  29.3 2.2 %shard_map.122 = (f32[6,8,8,512]{3,2,1,0:T(8,128)}, f32[3,8,8,512]{3,2,1,0:T(8,128)}, f32[3,512]{1,0:T(4,128)}) custom-call(f32[6,8,8,512]{3,2,1,0:T(8,128)} %get-tuple-element.9.stress, f32[3,512]{1,0:T(4,128)} %get-tuple-element.10.pushed, f32[3,8,8,512]{3,2,1,0:T(8,128)} %get-tuple-element.11.force_in, f32[3,8,512]{2,1,0:T(8,128)} %get-tuple-element.12.from_x_in, ...), custom_call_target="tpu_custom_call" | custom-call | tf_op jit(solution)/shard_map/pallas_call | solution.py:610
